TPU v7x, 32 devices: a whole 2x2x4 slice. The times are simulated.
32 devices in a mesh: dp: 8 (over z, core), pos: 4 (over y, x).
Axes of the slice: x: 2, y: 2, z: 4, core: 2. Of those that a mesh axis runs over, the one named last changes fastest.
Arguments:
- features: bfloat16 [64, 128, 224], P(('dp', 'pos')), may hold values from -6 to 6
- counts: int32 [32], P(('dp', 'pos')), may hold values from 1 to 2, as said below
- channel_order: int32 [224], replicated, may hold values from 0 to 223, each once
Outputs:
- mean: float32 [128, 100], P('pos')
- covariance: float32 [128, 100, 100], P('pos')
Inputs may be any that keep to these rules, and one draw needn't show every extreme that they name: `counts`: some device has all 2 slots live and some device only one.
All inputs are finite; a program needn't handle non-finite values.
Results may differ from a plain program's by a relative error of at most 0.0003.
Values may be sent and summed in bfloat16 or wider, within the bound.
No kernel may reach another device: no remote copies, remote signals or barrier semaphores. Data moves between devices by JAX's collectives and lax.ppermute only.
A program may use at most 128 MiB of HBM per device.

v0:
```python
import jax
import jax.numpy as jnp
from jax import lax
from jax.sharding import PartitionSpec as P

CH = 100


def local_stats(received, source_counts, slots, rows, width):
    sources = source_counts.shape[0]
    samples = received.reshape(sources * slots, rows, width).astype(jnp.float32)
    live_mask = (jnp.arange(slots, dtype=jnp.float32)[None, :] < source_counts[:, None]).astype(
        jnp.float32
    )
    live_mask = live_mask.reshape(sources * slots)
    group_count = jnp.sum(source_counts).reshape(1)
    group_sums = jnp.sum(samples, axis=0)
    group_mean = group_sums / group_count
    centered = (samples - group_mean[None]) * live_mask[:, None, None]
    products = jnp.einsum("gpc,gpd->pcd", centered, centered, precision=lax.Precision.HIGHEST)
    return (group_count, group_sums, group_mean, products)


def common_mean(group_count, group_sums, group_mean):
    total_count, total_sums = lax.psum((group_count, group_sums), "dp")
    mean = total_sums / total_count
    offset = group_mean - mean
    weighted = offset * group_count
    return (total_count, mean, offset, weighted)


def on_device(features, counts, channel_order):
    slots, positions, channels = features.shape
    groups = lax.axis_size("pos")
    pos_dev = positions // groups
    kept = channel_order[:CH]
    picker = (kept[None, :] == jnp.arange(channels, dtype=jnp.int32)[:, None]).astype(jnp.bfloat16)
    owned = counts[0]
    slot_live = (jnp.arange(slots, dtype=jnp.int32) < owned).astype(jnp.bfloat16)
    embed = jnp.dot(
        features.reshape(slots * positions, channels), picker, preferred_element_type=jnp.float32
    )
    embed = embed.astype(jnp.bfloat16).reshape(slots, positions, CH) * slot_live[:, None, None]
    identity = jnp.eye(CH, dtype=jnp.float32)
    packed = embed.reshape(slots, groups, pos_dev * CH)
    owned_wire = jnp.broadcast_to(owned.astype(jnp.bfloat16).reshape(1, 1, 1), (1, groups, 1))
    received, source_counts = (
        lax.all_to_all(packed, "pos", split_axis=1, concat_axis=0, tiled=True),
        lax.all_to_all(owned_wire, "pos", split_axis=1, concat_axis=0, tiled=True),
    )
    source_counts = source_counts.reshape(groups).astype(jnp.float32)
    group_count, group_sums, group_mean, products = local_stats(
        received, source_counts, slots, pos_dev, CH
    )
    total_count, mean, offset, weighted = common_mean(group_count, group_sums, group_mean)
    own_term = products + offset[:, :, None] * weighted[:, None, :]
    summed = lax.psum(own_term, "dp")
    covariance = summed / (total_count[0] - 1.0) + 0.01 * identity
    return (mean, covariance)


def solution(mesh):
    in_specs = (P(("dp", "pos"), None, None), P(("dp", "pos")), P())
    out_specs = (P("pos", None), P("pos", None, None))
    return jax.shard_map(
        on_device, mesh=mesh, in_specs=in_specs, out_specs=out_specs, check_vma=False
    )
```

profile of v0, /device:TPU:0, one launch (start us, length us, event | category | flops | bytes accessed | tf_op | source)
XLA Modules:
  0.0 129.7 jit_solution(13337276662901932767)
XLA Ops:
  7.2 0.0 copy-start
  7.9 0.6 broadcast_in_dim.2
  8.4 5.2 %all-to-all-start.1 = ((bf16[1,4,1]{2,0,1:T(2,128)(2,1)}), bf16[1,4,1]{2,0,1:T(2,128)(2,1)S(1)}, u32[]{:S(2)}, u32[]{:S(2)}) async-start(bf16[1,4,1]{2,0,1:T(2,128)(2,1)} %broadcast_in_dim.2), calls=%async_computation.1 | async-start | bytes 4096 | tf_op jit(solution)/shard_map/all_to_all | solution.py:49
  13.6 0.7 slice.3
  14.3 0.0 copy-done
  14.3 0.2 fusion
  14.5 0.1 copy.19
  14.6 0.2 reshape.81
  14.8 0.1 broadcast_multiply_fusion
  14.9 0.7 copy.20
  15.6 2.6 %all-to-all-done.1 = bf16[1,4,1]{2,0,1:T(2,128)(2,1)S(1)} async-done(((bf16[1,4,1]{2,0,1:T(2,128)(2,1)}), bf16[1,4,1]{2,0,1:T(2,128)(2,1)S(1)}, u32[]{:S(2)}, u32[]{:S(2)}) %all-to-all-start.1) | async-done | bytes 40 | tf_op jit(solution)/shard_map/all_to_all | solution.py:49
  18.2 3.3 %all-to-all-start = ((bf16[2,4,3200]{2,0,1:T(2,128)(2,1)}), bf16[2,4,3200]{2,0,1:T(2,128)(2,1)S(1)}, u32[]{:S(2)}, u32[]{:S(2)}) async-start(bf16[2,4,3200]{2,0,1:T(2,128)(2,1)} %copy.20), calls=%async_computation | async-start | bytes 102400 | tf_op jit(solution)/shard_map/all_to_all | solution.py:48
  21.5 0.0 all-reduce.3.cloned.1.call-start
  21.5 0.7 convert_reduce_fusion.1
  22.2 0.1 fusion.6
  22.3 0.1 reshape.85
  22.4 3.9 %all-to-all-done = bf16[2,4,3200]{2,0,1:T(2,128)(2,1)S(1)} async-done(((bf16[2,4,3200]{2,0,1:T(2,128)(2,1)}), bf16[2,4,3200]{2,0,1:T(2,128)(2,1)S(1)}, u32[]{:S(2)}, u32[]{:S(2)}) %all-to-all-start) | async-done | bytes 51232 | tf_op jit(solution)/shard_map/all_to_all | solution.py:48
  26.2 0.1 convert_reduce_fusion
  26.3 0.1 reduce_sum.21
  26.5 0.3 reshape.84
  26.7 27.4 %all-reduce = (f32[32,100]{1,0:T(8,128)S(1)}, f32[]{:T(128)}) all-reduce(f32[32,100]{1,0:T(8,128)S(1)} %reduce_sum.21, f32[]{:T(128)} %get-tuple-element.11), channel_id=1, replica_groups=mesh['dp'=8,'pos'=4] {'dp'}, use_global_device_ids=true, to_apply=%region_1.0 | all-reduce | flops 3201 | bytes 25608 | tf_op jit(solution)/shard_map/psum | solution.py:25
  54.2 1.9 %broadcast_multiply_fusion.1 = (f32[32,100]{1,0:T(8,128)S(1)}, f32[32,100]{1,0:T(8,128)S(1)}, f32[32,100]{1,0:T(8,128)S(1)}, f32[32,100]{1,0:T(8,128)}) fusion(f32[]{:T(128)} %get-tuple-element.11, f32[32,100]{1,0:T(8,128)S(1)} %reduce_sum.21, f32[32,100]{1,0:T(8,128)S(1)} %get-tuple-element.12, f32[]{:T(128)} %get-tuple-element.13), kind=kLoop, calls=%fused_computation.15 | loop fusion | flops 12800 | bytes 76808 | tf_op jit(solution)/shard_map/mul | solution.py:28
  56.1 0.1 subtract_multiply_fusion
  56.2 4.4 %multiply_add_fusion = f32[32,100,100]{2,1,0:T(8,128)} fusion(f32[32,100]{1,0:T(8,128)S(1)} %get-tuple-element.14, f32[32,100]{1,0:T(8,128)S(1)} %get-tuple-element.15, f32[8,32,100]{2,1,0:T(8,128)S(1)} %subtract_multiply_fusion), kind=kOutput, calls=%fused_computation.1 | convolution fusion | flops 31360000 | bytes 1408000 | tf_op jit(solution)/shard_map/gpc,gpd->pcd/dot_general | solution.py:20
  60.6 0.0 all-reduce.3.cloned.1.call-update
  61.3 58.5 %all-reduce.3.cloned.1.call-done = f32[32,100,100]{2,1,0:T(8,128)} async-done(((f32[32,100,100]{2,1,0:T(8,128)}), f32[32,100,100]{2,1,0:T(8,128)}) %all-reduce.3.cloned.1.call-update) | async-done | bytes 1280016 | tf_op jit(solution)/shard_map/psum | solution.py:57
  119.8 1.6 %divide_add_fusion = f32[32,100,100]{2,1,0:T(8,128)S(1)} fusion(f32[32,100,100]{2,1,0:T(8,128)} %all-reduce.3.cloned.1.call-done, f32[100,100]{1,0:T(8,128)S(1)} %fusion.5, f32[]{:T(128)S(6)} %sub.17), kind=kLoop, calls=%fused_computation | loop fusion | flops 640000 | bytes 2600004 | tf_op jit(solution)/shard_map/add | solution.py:58
  121.4 1.5 %copy.23 = f32[32,100,100]{2,0,1:T(8,128)} copy(f32[32,100,100]{2,1,0:T(8,128)S(1)} %divide_add_fusion) | data formatting | bytes 2560000
  (3 shorter events, 0.1 us)
Async XLA Ops:
  7.2 7.1 %copy-start = (bf16[2,128,224]{1,2,0:T(8,128)(2,1)S(1)}, bf16[2,128,224]{1,2,0:T(8,128)(2,1)}, u32[]{:S(2)}) copy-start(bf16[2,128,224]{1,2,0:T(8,128)(2,1)} %param.3) | copy-start | bytes 344068
  8.4 9.7 %all-to-all-start.1 = ((bf16[1,4,1]{2,0,1:T(2,128)(2,1)}), bf16[1,4,1]{2,0,1:T(2,128)(2,1)S(1)}, u32[]{:S(2)}, u32[]{:S(2)}) async-start(bf16[1,4,1]{2,0,1:T(2,128)(2,1)} %broadcast_in_dim.2), calls=%async_computation.1 | async-start | bytes 4096 | tf_op jit(solution)/shard_map/all_to_all | solution.py:49
  18.2 8.1 %all-to-all-start = ((bf16[2,4,3200]{2,0,1:T(2,128)(2,1)}), bf16[2,4,3200]{2,0,1:T(2,128)(2,1)S(1)}, u32[]{:S(2)}, u32[]{:S(2)}) async-start(bf16[2,4,3200]{2,0,1:T(2,128)(2,1)} %copy.20), calls=%async_computation | async-start | bytes 102400 | tf_op jit(solution)/shard_map/all_to_all | solution.py:48
  21.5 98.3 %all-reduce.3.cloned.1.call-start = ((), (), s32[]{:S(2)}) async-start(), calls=%async_computation.2 | async-start | bytes 3407872 | tf_op jit(solution)/shard_map/psum | solution.py:57
Sparse Core Ops, SparseCore 0:
  60.7 59.0 all-reduce.2
where the time goes:
time: 130 us
  waiting for transfers between devices  65 us (50%)
  blocking collectives  27.4 us (21%)
  between operations  15.4 us (12%)
  starting transfers between devices  8.48 us (7%)
  other arithmetic  4.59 us (4%)
  matrix products  4.57 us (4%)
  local copies, waits for them, and re-layouts  4.13 us (3%)
    psum x1, waiting for transfers between devices, on_device(): summed = lax.psum(own_term, 'dp')  58.5 us
    psum x1, blocking collectives, common_mean(): total_count, total_sums = lax.psum((group_count, group_sums), 'dp')  27.4 us
    all_to_all x1, starting transfers between devices, on_device(): lax.all_to_all(owned_wire, 'pos', split_axis=1, concat_axis=0, tiled=True)  5.16 us
    dot_general x1, matrix products, local_stats(): jnp.einsum('gpc,gpd->pcd', centered, centered, precision=lax.Precision.HI...  4.36 us
    all_to_all x1, waiting for transfers between devices, on_device(): lax.all_to_all(packed, 'pos', split_axis=1, concat_axis=0, tiled=True)  3.88 us
    all_to_all x1, starting transfers between devices, on_device(): lax.all_to_all(packed, 'pos', split_axis=1, concat_axis=0, tiled=True)  3.28 us
    all_to_all x1, waiting for transfers between devices, on_device(): lax.all_to_all(owned_wire, 'pos', split_axis=1, concat_axis=0, tiled=True)  2.61 us
  transfers between devices with their start and end apart: 3, of which 3 were waited for; matrix products, arithmetic and copies ran while one was open for 2% of the time, Pallas kernels for 0%

commit v1 on v0

v1 whole, which is shorter than its diff:
```python
import functools

import jax
import jax.numpy as jnp
from jax import lax
from jax.experimental import pallas as pl
from jax.experimental.pallas import tpu as pltpu
from jax.sharding import PartitionSpec as P

CH = 100
CORES = 2
LANES = 128
MIB = 1 << 20


def partner(n, step):
    if n & (n - 1) == 0:
        return [(i, i ^ step) for i in range(n)]
    return [(i, (i + step) % n) for i in range(n)]


def shift(index, n, step, sign):
    if n & (n - 1) == 0:
        return index ^ step
    return lax.rem(index + sign * step + n, n)


def select_kernel(groups, pos_dev, order_ref, counts_ref, features_ref, *out_refs):
    slots, channels, positions = features_ref.shape
    me = lax.axis_index("pos")
    order = order_ref[...].reshape(1, channels)[:, :LANES]
    lane = lax.broadcasted_iota(jnp.int32, (channels, LANES), 1)
    row = lax.broadcasted_iota(jnp.int32, (channels, LANES), 0)
    picker = jnp.where((row == order) & (lane < CH), 1.0, 0.0).astype(jnp.bfloat16)
    flag = lax.broadcasted_iota(jnp.int32, (positions, LANES), 1) == CH
    owned = counts_ref[0]
    scratch = out_refs[-1]
    for slot in range(slots):
        picked = lax.dot_general(
            features_ref[slot], picker, (((0,), (0,)), ((), ())), preferred_element_type=jnp.float32
        )
        picked = jnp.where(flag, 1.0, picked)
        live = jnp.where(slot < owned, 1.0, 0.0)
        scratch[slot] = picked * live
    for step in range(groups):
        begin = pl.multiple_of(shift(me, groups, step, 1) * pos_dev, pos_dev)
        for slot in range(slots):
            out_refs[step][pl.ds(slot * pos_dev, pos_dev), :] = scratch[
                slot, pl.ds(begin, pos_dev), :
            ].astype(jnp.bfloat16)


def merge_kernel(slots, pos_dev, *refs):
    *in_refs, out_ref, scratch = refs
    images = len(in_refs) * slots
    for source, ref in enumerate(in_refs):
        block = ref[...].astype(jnp.float32)
        for slot in range(slots):
            scratch[pl.ds(source * slots + slot, pos_dev, stride=images), :] = block[
                slot * pos_dev : (slot + 1) * pos_dev
            ]
    out_ref[...] = scratch[...].astype(jnp.bfloat16)


def stats_kernel(images, rows, depth, *refs):
    *in_refs, mean_ref, cov_ref, held = refs
    blocks = len(in_refs)
    me = lax.axis_index("dp")
    for step, ref in enumerate(in_refs):
        z_step, c_step = step // CORES, step % CORES
        owner = shift(me // CORES, depth, z_step, -1) * CORES + ((me % CORES) ^ c_step)
        held[owner] = ref[...].astype(jnp.float32).reshape(rows, images, LANES)
    everyone = blocks * images
    live = jnp.broadcast_to(
        held[:, 0].reshape(everyone, LANES)[:, CH : CH + 1], (everyone, LANES)
    )
    total = jnp.sum(live, axis=0, keepdims=True)
    factor = 1.0 / (total - 1.0)
    eye = lax.broadcasted_iota(jnp.int32, (LANES, LANES), 0) == lax.broadcasted_iota(
        jnp.int32, (LANES, LANES), 1
    )
    ridge = jnp.where(eye, 0.01, 0.0)
    for position in range(rows):
        samples = held[:, position].reshape(everyone, LANES)
        mean = jnp.sum(samples, axis=0, keepdims=True) / total
        mean_ref[pl.ds(position, 1), :] = mean[:, :CH]
        centered = samples - mean * live
        high = centered.astype(jnp.bfloat16)
        low = (centered - high.astype(jnp.float32)).astype(jnp.bfloat16)
        sums = lax.dot_general(
            jnp.concatenate([high, high, low], axis=0),
            jnp.concatenate([high, low, high], axis=0),
            (((0,), (0,)), ((), ())),
            preferred_element_type=jnp.float32,
        )
        cov_ref[:, position, :] = (sums * factor + ridge)[:CH, :CH]


def on_device(features, counts, channel_order):
    slots, positions, channels = features.shape
    groups, dp = lax.axis_size("pos"), lax.axis_size("dp")
    depth = dp // CORES
    pos_dev = positions // groups
    images = groups * slots
    wire = jnp.bfloat16
    vmem = pl.BlockSpec(memory_space=pltpu.VMEM)

    parts = pl.pallas_call(
        functools.partial(select_kernel, groups, pos_dev),
        out_shape=[jax.ShapeDtypeStruct((slots * pos_dev, LANES), wire)] * groups,
        in_specs=[vmem, pl.BlockSpec(memory_space=pltpu.SMEM), vmem],
        out_specs=[vmem] * groups,
        scratch_shapes=[pltpu.VMEM((slots, positions, LANES), jnp.float32)],
        compiler_params=pltpu.CompilerParams(vmem_limit_bytes=16 * MIB),
    )(channel_order, counts, jnp.transpose(features, (0, 2, 1)))

    got = [parts[0]] + [
        lax.ppermute(parts[step], "pos", partner(groups, step)) for step in range(1, groups)
    ]

    own = pl.pallas_call(
        functools.partial(merge_kernel, slots, pos_dev),
        out_shape=jax.ShapeDtypeStruct((pos_dev * images, LANES), wire),
        in_specs=[vmem] * groups,
        out_specs=vmem,
        scratch_shapes=[pltpu.VMEM((pos_dev * images, LANES), jnp.float32)],
        compiler_params=pltpu.CompilerParams(vmem_limit_bytes=16 * MIB),
    )(*got)

    blocks = {}
    swap = [(i, i ^ 1) for i in range(dp)]
    order = sorted(range(1, depth), reverse=True)
    blocks[0] = own
    for step in order:
        pairs = [
            (a * CORES + c, b * CORES + c) for a, b in partner(depth, step) for c in range(CORES)
        ]
        blocks[step] = lax.ppermute(own, "dp", pairs)
    arrays = []
    for step in range(depth):
        arrays += [blocks[step], lax.ppermute(blocks[step], "dp", swap)]

    rows = 8
    mean, covariance = pl.pallas_call(
        functools.partial(stats_kernel, images, rows, depth),
        grid=(pos_dev // rows,),
        out_shape=[
            jax.ShapeDtypeStruct((pos_dev, CH), jnp.float32),
            jax.ShapeDtypeStruct((CH, pos_dev, CH), jnp.float32),
        ],
        in_specs=[pl.BlockSpec((rows * images, LANES), lambda g: (g, 0))] * dp,
        out_specs=[
            pl.BlockSpec((rows, CH), lambda g: (g, 0)),
            pl.BlockSpec((CH, rows, CH), lambda g: (0, g, 0)),
        ],
        scratch_shapes=[pltpu.VMEM((dp, rows, images, LANES), jnp.float32)],
        compiler_params=pltpu.CompilerParams(vmem_limit_bytes=48 * MIB),
    )(*arrays)
    return mean, jnp.transpose(covariance, (1, 0, 2))


def solution(mesh):
    in_specs = (P(("dp", "pos"), None, None), P(("dp", "pos")), P())
    out_specs = (P("pos", None), P("pos", None, None))
    return jax.shard_map(
        on_device, mesh=mesh, in_specs=in_specs, out_specs=out_specs, check_vma=False
    )
```

time: 130 us -> 26 us (0.20)
  waiting for transfers between devices: 65 us -> 9.89 us
  blocking collectives: 27.4 us -> 0 us
  between operations: 15.4 us -> 1.31 us
  other arithmetic: 4.59 us -> 0 us
  matrix products: 4.57 us -> 0 us
  Pallas kernels: 0 us -> 3.56 us
  local copies, waits for them, and re-layouts: 4.13 us -> 1.57 us
    psum x1 -> x0, waiting for transfers between devices: 58.5 us -> none  [on_device(): summed = lax.psum(own_term, 'dp')]
    psum x1 -> x0, blocking collectives: 27.4 us -> none  [common_mean(): total_count, total_sums = lax.psum((group_count, group_sums), 'dp')]
    ppermute x0 -> x10, waiting for transfers between devices: none -> 9.89 us  [the longest x3 4.62 us: on_device(): lax.ppermute(parts[step], 'pos', partner(groups, step))]
    ppermute x0 -> x10, starting transfers between devices: none -> 9.51 us  [the longest x3 4.54 us: on_device(): lax.ppermute(parts[step], 'pos', partner(groups, step))]
    all_to_all x2 -> x0, starting transfers between devices: 8.44 us -> none  [the longest x1 5.16 us: on_device(): lax.all_to_all(owned_wire, 'pos', split_axis=1, concat_axis=0, tiled=True)]
    all_to_all x2 -> x0, waiting for transfers between devices: 6.49 us -> none  [the longest x1 3.88 us: on_device(): lax.all_to_all(packed, 'pos', split_axis=1, concat_axis=0, tiled=True)]
    dot_general x2 -> x0, matrix products: 4.57 us -> none  [the longest x1 4.36 us: local_stats(): jnp.einsum('gpc,gpd->pcd', centered, centered, precision=lax.Precision.HI...]
    pallas_call x0 -> x3, Pallas kernels: none -> 3.56 us  [the longest x1 3.29 us: on_device(): pl.pallas_call(functools.partial(stats_kernel, images, rows, depth), grid...]
  transfers between devices with their start and end apart: 3 -> 10, of which waited for: 3 -> 7; matrix products, arithmetic and copies ran while one was open for 2% -> 0% of each run, Pallas kernels for 0% -> 0%
where the time goes in v1:
time: 26 us; the launch traced here: 25.8 us
  waiting for transfers between devices  9.89 us (38%)
  starting transfers between devices  9.51 us (37%)
  Pallas kernels  3.56 us (14%)
  local copies, waits for them, and re-layouts  1.57 us (6%)
  between operations  1.31 us (5%)
    ppermute x3, waiting for transfers between devices, on_device(): lax.ppermute(parts[step], 'pos', partner(groups, step))  4.62 us
    ppermute x3, starting transfers between devices, on_device(): lax.ppermute(parts[step], 'pos', partner(groups, step))  4.54 us
    ppermute x3, starting transfers between devices, on_device(): blocks[step] = lax.ppermute(own, 'dp', pairs)  4.45 us
    ppermute x3, waiting for transfers between devices, on_device(): blocks[step] = lax.ppermute(own, 'dp', pairs)  4.38 us
    pallas_call x1, Pallas kernels, on_device(): pl.pallas_call(functools.partial(stats_kernel, images, rows, depth), grid...  3.29 us
    unnamed x4, local copies, waits for them, and re-layouts  1.57 us
    ppermute x4, waiting for transfers between devices, on_device(): arrays += [blocks[step], lax.ppermute(blocks[step], 'dp', swap)]  0.9 us
  transfers between devices with their start and end apart: 10, of which 7 were waited for; matrix products, arithmetic and copies ran while one was open for 0% of the time, Pallas kernels for 0%

profile of v1, /device:TPU:0, one launch (start us, length us, event | category | flops | bytes accessed | tf_op | source)
XLA Modules:
  0.0 25.8 jit_solution(3358081749024179483)
XLA Ops:
  1.3 0.0 copy-start
  1.3 0.9 %copy-done = bf16[2,128,224]{1,2,0:T(8,128)(2,1)S(1)} copy-done((bf16[2,128,224]{1,2,0:T(8,128)(2,1)S(1)}, bf16[2,128,224]{1,2,0:T(8,128)(2,1)}, u32[]{:S(2)}) %copy-start) | copy-done | bytes 114712
  2.2 0.0 copy-start.1
  2.2 0.7 %copy-done.1 = s32[224]{0:T(256)S(1)} copy-done((s32[224]{0:T(256)S(1)}, s32[224]{0:T(256)}, u32[]{:S(2)}) %copy-start.1) | copy-done | bytes 920
  2.9 0.2 shard_map.50
  3.1 3.0 %collective-permute-start = (bf16[64,128]{1,0:T(8,128)(2,1)S(1)}, bf16[64,128]{1,0:T(8,128)(2,1)S(1)}, u32[]{:S(2)}, u32[]{:S(2)}) collective-permute-start(bf16[64,128]{1,0:T(8,128)(2,1)S(1)} %get-tuple-element.9), channel_id=1, source_target_pairs={{0,1},{1,0},{2,3},{3,2},{4,5},{5,4},{6,7},{7,6},{8,9},{9,8},{10,11... | collective-permute-start | bytes 49160 | tf_op jit(solution)/shard_map/ppermute | solution.py:118
  6.1 1.5 %collective-permute-start.1 = (bf16[64,128]{1,0:T(8,128)(2,1)S(1)}, bf16[64,128]{1,0:T(8,128)(2,1)S(1)}, u32[]{:S(2)}, u32[]{:S(2)}) collective-permute-start(bf16[64,128]{1,0:T(8,128)(2,1)S(1)} %get-tuple-element.10), channel_id=1, source_target_pairs={{0,2},{1,3},{2,0},{3,1},{4,6},{5,7},{6,4},{7,5},{8,10},{9,11},{10,... | collective-permute-start | bytes 49160 | tf_op jit(solution)/shard_map/ppermute | solution.py:118
  7.6 0.0 collective-permute-start.2
  7.6 0.2 collective-permute-done.refs_1_
  7.8 2.0 %collective-permute-done.1.refs_2_ = bf16[64,128]{1,0:T(8,128)(2,1)S(1)} collective-permute-done((bf16[64,128]{1,0:T(8,128)(2,1)S(1)}, bf16[64,128]{1,0:T(8,128)(2,1)S(1)}, u32[]{:S(2)}, u32[]{:S(2)}) %collective-permute-start.1) | collective-permute-done | bytes 16416 | tf_op jit(solution)/shard_map/ppermute | solution.py:118
  9.8 2.4 %collective-permute-done.2.refs_3_ = bf16[64,128]{1,0:T(8,128)(2,1)S(1)} collective-permute-done((bf16[64,128]{1,0:T(8,128)(2,1)S(1)}, bf16[64,128]{1,0:T(8,128)(2,1)S(1)}, u32[]{:S(2)}, u32[]{:S(2)}) %collective-permute-start.2) | collective-permute-done | bytes 16416 | tf_op jit(solution)/shard_map/ppermute | solution.py:118
  12.3 3.7 %collective-permute-start.8 = (bf16[256,128]{1,0:T(8,128)(2,1)S(1)}, bf16[256,128]{1,0:T(8,128)(2,1)S(1)}, u32[]{:S(2)}, u32[]{:S(2)}) collective-permute-start(bf16[256,128]{1,0:T(8,128)(2,1)S(1)} %shard_map.51.refs_0_), channel_id=1, source_target_pairs={{0,24},{4,28},{8,16},{12,20},{16,8},{20,12},{24,0},{28,4},{1,25},{... | collective-permute-start | bytes 196616 | tf_op jit(solution)/shard_map/ppermute | solution.py:138
  16.0 0.0 collective-permute-start.6
  16.0 0.8 %collective-permute-start.4 = (bf16[256,128]{1,0:T(8,128)(2,1)S(1)}, bf16[256,128]{1,0:T(8,128)(2,1)S(1)}, u32[]{:S(2)}, u32[]{:S(2)}) collective-permute-start(bf16[256,128]{1,0:T(8,128)(2,1)S(1)} %shard_map.51.refs_0_), channel_id=1, source_target_pairs={{0,8},{4,12},{8,0},{12,4},{16,24},{20,28},{24,16},{28,20},{1,9},{5... | collective-permute-start | bytes 196616 | tf_op jit(solution)/shard_map/ppermute | solution.py:138
  16.7 0.0 collective-permute-start.3
  16.8 1.8 %collective-permute-done.8.refs_6_ = bf16[256,128]{1,0:T(8,128)(2,1)S(1)} collective-permute-done((bf16[256,128]{1,0:T(8,128)(2,1)S(1)}, bf16[256,128]{1,0:T(8,128)(2,1)S(1)}, u32[]{:S(2)}, u32[]{:S(2)}) %collective-permute-start.8) | collective-permute-done | bytes 65568 | tf_op jit(solution)/shard_map/ppermute | solution.py:138
  18.5 0.0 collective-permute-start.9
  18.5 2.6 %collective-permute-done.6.refs_4_ = bf16[256,128]{1,0:T(8,128)(2,1)S(1)} collective-permute-done((bf16[256,128]{1,0:T(8,128)(2,1)S(1)}, bf16[256,128]{1,0:T(8,128)(2,1)S(1)}, u32[]{:S(2)}, u32[]{:S(2)}) %collective-permute-start.6) | collective-permute-done | bytes 65568 | tf_op jit(solution)/shard_map/ppermute | solution.py:138
  21.1 0.0 collective-permute-start.7
  21.1 0.0 collective-permute-done.4.refs_2_
  21.1 0.5 %collective-permute-start.5 = (bf16[256,128]{1,0:T(8,128)(2,1)S(1)}, bf16[256,128]{1,0:T(8,128)(2,1)S(1)}, u32[]{:S(2)}, u32[]{:S(2)}) collective-permute-start(bf16[256,128]{1,0:T(8,128)(2,1)S(1)} %collective-permute-done.4.refs_2_), channel_id=1, source_target_pairs={{0,4},{4,0},{8,12},{12,8},{16,20},{20,16},{24,28},{28,24},{1,5},{5... | collective-permute-start | bytes 196616 | tf_op jit(solution)/shard_map/ppermute | solution.py:141
  21.6 0.0 collective-permute-done.3.refs_1_
  21.6 0.0 collective-permute-done.9.refs_7_
  21.6 0.7 %collective-permute-done.7.refs_5_ = bf16[256,128]{1,0:T(8,128)(2,1)S(1)} collective-permute-done((bf16[256,128]{1,0:T(8,128)(2,1)S(1)}, bf16[256,128]{1,0:T(8,128)(2,1)S(1)}, u32[]{:S(2)}, u32[]{:S(2)}) %collective-permute-start.7) | collective-permute-done | bytes 65568 | tf_op jit(solution)/shard_map/ppermute | solution.py:141
  22.4 0.2 collective-permute-done.5.refs_3_
  22.5 3.3 %shard_map.52 = (f32[32,100]{1,0:T(8,128)}, f32[100,32,100]{2,1,0:T(8,128)}) custom-call(bf16[256,128]{1,0:T(8,128)(2,1)S(1)} %shard_map.51.refs_0_, bf16[256,128]{1,0:T(8,128)(2,1)S(1)} %collective-permute-done.3.refs_1_, bf16[256,128]{1,0:T(8,128)(2,1)S(1)} %collective-permute-done.4.refs_2_, bf16[256,128]{1,0:T(8,128)(2,1)S(1)} %collective-permute-done.5.refs_3_, ...), custom_call_target="tpu_custom_call" | custom-call | tf_op jit(solution)/shard_map/pallas_call | solution.py:144
  (1 shorter events, 0.0 us)
Async XLA Ops:
  1.3 0.9 %copy-start = (bf16[2,128,224]{1,2,0:T(8,128)(2,1)S(1)}, bf16[2,128,224]{1,2,0:T(8,128)(2,1)}, u32[]{:S(2)}) copy-start(bf16[2,128,224]{1,2,0:T(8,128)(2,1)} %param.3) | copy-start | bytes 344068
  2.2 0.7 %copy-start.1 = (s32[224]{0:T(256)S(1)}, s32[224]{0:T(256)}, u32[]{:S(2)}) copy-start(s32[224]{0:T(256)} %order_ref.1) | copy-start | bytes 2692
  3.1 4.7 %collective-permute-start = (bf16[64,128]{1,0:T(8,128)(2,1)S(1)}, bf16[64,128]{1,0:T(8,128)(2,1)S(1)}, u32[]{:S(2)}, u32[]{:S(2)}) collective-permute-start(bf16[64,128]{1,0:T(8,128)(2,1)S(1)} %get-tuple-element.9), channel_id=1, source_target_pairs={{0,1},{1,0},{2,3},{3,2},{4,5},{5,4},{6,7},{7,6},{8,9},{9,8},{10,11... | collective-permute-start | bytes 49160 | tf_op jit(solution)/shard_map/ppermute | solution.py:118
  6.1 3.7 %collective-permute-start.1 = (bf16[64,128]{1,0:T(8,128)(2,1)S(1)}, bf16[64,128]{1,0:T(8,128)(2,1)S(1)}, u32[]{:S(2)}, u32[]{:S(2)}) collective-permute-start(bf16[64,128]{1,0:T(8,128)(2,1)S(1)} %get-tuple-element.10), channel_id=1, source_target_pairs={{0,2},{1,3},{2,0},{3,1},{4,6},{5,7},{6,4},{7,5},{8,10},{9,11},{10,... | collective-permute-start | bytes 49160 | tf_op jit(solution)/shard_map/ppermute | solution.py:118
  7.6 4.6 %collective-permute-start.2 = (bf16[64,128]{1,0:T(8,128)(2,1)S(1)}, bf16[64,128]{1,0:T(8,128)(2,1)S(1)}, u32[]{:S(2)}, u32[]{:S(2)}) collective-permute-start(bf16[64,128]{1,0:T(8,128)(2,1)S(1)} %get-tuple-element.11), channel_id=1, source_target_pairs={{0,3},{1,2},{2,1},{3,0},{4,7},{5,6},{6,5},{7,4},{8,11},{9,10},{10,... | collective-permute-start | bytes 49160 | tf_op jit(solution)/shard_map/ppermute | solution.py:118
  12.3 6.2 %collective-permute-start.8 = (bf16[256,128]{1,0:T(8,128)(2,1)S(1)}, bf16[256,128]{1,0:T(8,128)(2,1)S(1)}, u32[]{:S(2)}, u32[]{:S(2)}) collective-permute-start(bf16[256,128]{1,0:T(8,128)(2,1)S(1)} %shard_map.51.refs_0_), channel_id=1, source_target_pairs={{0,24},{4,28},{8,16},{12,20},{16,8},{20,12},{24,0},{28,4},{1,25},{... | collective-permute-start | bytes 196616 | tf_op jit(solution)/shard_map/ppermute | solution.py:138
  16.0 5.2 %collective-permute-start.6 = (bf16[256,128]{1,0:T(8,128)(2,1)S(1)}, bf16[256,128]{1,0:T(8,128)(2,1)S(1)}, u32[]{:S(2)}, u32[]{:S(2)}) collective-permute-start(bf16[256,128]{1,0:T(8,128)(2,1)S(1)} %shard_map.51.refs_0_), channel_id=1, source_target_pairs={{0,16},{4,20},{8,24},{12,28},{16,0},{20,4},{24,8},{28,12},{1,17},{... | collective-permute-start | bytes 196616 | tf_op jit(solution)/shard_map/ppermute | solution.py:138
  16.0 5.2 %collective-permute-start.4 = (bf16[256,128]{1,0:T(8,128)(2,1)S(1)}, bf16[256,128]{1,0:T(8,128)(2,1)S(1)}, u32[]{:S(2)}, u32[]{:S(2)}) collective-permute-start(bf16[256,128]{1,0:T(8,128)(2,1)S(1)} %shard_map.51.refs_0_), channel_id=1, source_target_pairs={{0,8},{4,12},{8,0},{12,4},{16,24},{20,28},{24,16},{28,20},{1,9},{5... | collective-permute-start | bytes 196616 | tf_op jit(solution)/shard_map/ppermute | solution.py:138
  16.7 4.9 %collective-permute-start.3 = (bf16[256,128]{1,0:T(8,128)(2,1)S(1)}, bf16[256,128]{1,0:T(8,128)(2,1)S(1)}, u32[]{:S(2)}, u32[]{:S(2)}) collective-permute-start(bf16[256,128]{1,0:T(8,128)(2,1)S(1)} %shard_map.51.refs_0_), channel_id=1, source_target_pairs={{0,4},{4,0},{8,12},{12,8},{16,20},{20,16},{24,28},{28,24},{1,5},{5... | collective-permute-start | bytes 196616 | tf_op jit(solution)/shard_map/ppermute | solution.py:141
  18.5 3.1 %collective-permute-start.9 = (bf16[256,128]{1,0:T(8,128)(2,1)S(1)}, bf16[256,128]{1,0:T(8,128)(2,1)S(1)}, u32[]{:S(2)}, u32[]{:S(2)}) collective-permute-start(bf16[256,128]{1,0:T(8,128)(2,1)S(1)} %collective-permute-done.8.refs_6_), channel_id=1, source_target_pairs={{0,4},{4,0},{8,12},{12,8},{16,20},{20,16},{24,28},{28,24},{1,5},{5... | collective-permute-start | bytes 196616 | tf_op jit(solution)/shard_map/ppermute | solution.py:141
  21.1 1.3 %collective-permute-start.7 = (bf16[256,128]{1,0:T(8,128)(2,1)S(1)}, bf16[256,128]{1,0:T(8,128)(2,1)S(1)}, u32[]{:S(2)}, u32[]{:S(2)}) collective-permute-start(bf16[256,128]{1,0:T(8,128)(2,1)S(1)} %collective-permute-done.6.refs_4_), channel_id=1, source_target_pairs={{0,4},{4,0},{8,12},{12,8},{16,20},{20,16},{24,28},{28,24},{1,5},{5... | collective-permute-start | bytes 196616 | tf_op jit(solution)/shard_map/ppermute | solution.py:141
  21.1 1.4 %collective-permute-start.5 = (bf16[256,128]{1,0:T(8,128)(2,1)S(1)}, bf16[256,128]{1,0:T(8,128)(2,1)S(1)}, u32[]{:S(2)}, u32[]{:S(2)}) collective-permute-start(bf16[256,128]{1,0:T(8,128)(2,1)S(1)} %collective-permute-done.4.refs_2_), channel_id=1, source_target_pairs={{0,4},{4,0},{8,12},{12,8},{16,20},{20,16},{24,28},{28,24},{1,5},{5... | collective-permute-start | bytes 196616 | tf_op jit(solution)/shard_map/ppermute | solution.py:141

commit v2 on v0

v2 whole, which is shorter than its diff:
```python
import functools

import jax
import jax.numpy as jnp
from jax import lax
from jax.experimental import pallas as pl
from jax.experimental.pallas import tpu as pltpu
from jax.sharding import PartitionSpec as P

CH = 100
CORES = 2
LANES = 128
ROWS = 8
PITCH = ROWS + 1
MIB = 1 << 20


def shift(index, n, step, sign=1):
    if n & (n - 1) == 0:
        return index ^ step
    return (index + sign * step + n) % n


def halves(n):
    small = max(f for f in range(1, n + 1) if n % f == 0 and f * f <= n)
    return small, n // small


def far_first(n_pos, n_z):
    steps = [(p, z) for p in range(n_pos) for z in range(n_z)]
    return sorted(steps, key=sum, reverse=True)[:-1]


def coordinates(dp, pos, dims):
    z_low, pos_low = dims
    z = dp // CORES
    return z // z_low, z % z_low, dp % CORES, pos // pos_low, pos % pos_low


def select_kernel(dims, pos_dev, features_hbm, counts_hbm, order_hbm, *refs):
    pos_low, pos_high = dims
    *out_refs, features_ref, counts_ref, order_ref, picked_ref, sems = refs
    copies = [
        pltpu.make_async_copy(source, target, sems.at[i])
        for i, (source, target) in enumerate(
            ((features_hbm, features_ref), (order_hbm, order_ref), (counts_hbm, counts_ref))
        )
    ]
    for copy in copies:
        copy.start()
    slots, channels, positions = features_ref.shape
    x = lax.axis_index("pos") % pos_low
    lane = lax.broadcasted_iota(jnp.int32, (channels, LANES), 1)
    row = lax.broadcasted_iota(jnp.int32, (channels, LANES), 0)
    flag = lax.broadcasted_iota(jnp.int32, (positions, LANES), 1) == CH
    for copy in reversed(copies):
        copy.wait()
    order = order_ref[...].reshape(1, channels)[:, :LANES]
    picker = jnp.where((row == order) & (lane < CH), 1.0, 0.0).astype(jnp.bfloat16)
    owned = counts_ref[0]
    for slot in range(slots):
        picked = lax.dot_general(
            features_ref[slot], picker, (((0,), (0,)), ((), ())), preferred_element_type=jnp.float32
        )
        picked = jnp.where(flag, 1.0, picked)
        picked_ref[slot] = picked * jnp.where(slot < owned, 1.0, 0.0)
    for step, out_ref in enumerate(out_refs):
        for high in range(pos_high):
            begin = (high * pos_low + shift(x, pos_low, step)) * pos_dev
            begin = pl.multiple_of(begin, pos_dev)
            for slot in range(slots):
                out_ref[pl.ds((high * slots + slot) * pos_dev, pos_dev), :] = picked_ref[
                    slot, pl.ds(begin, pos_dev), :
                ].astype(jnp.bfloat16)


def merge_kernel(dims, slots, pos_dev, *refs):
    z_low, z_high, pos_low, pos_high = dims
    in_refs, out_refs, scratch = refs[: pos_low * z_high], refs[pos_low * z_high : -1], refs[-1]
    z, _, _, y, _ = coordinates(lax.axis_index("dp"), lax.axis_index("pos"), (z_low, pos_low))
    images = len(in_refs) * slots
    size = slots * pos_dev
    for step, out_ref in enumerate(out_refs):
        begin = pl.multiple_of(shift(y, pos_high, step) * size, size)
        for source, ref in enumerate(in_refs):
            pos_step, z_step = source // z_high, source % z_high
            owner = shift(z, z_high, z_step, -1) * pos_low + pos_step
            block = ref[pl.ds(begin, size), :].astype(jnp.float32)
            for slot in range(slots):
                scratch[step, pl.ds(owner * slots + slot, pos_dev, stride=images), :] = block[
                    slot * pos_dev : (slot + 1) * pos_dev
                ]
        out_ref[...] = scratch[step].astype(jnp.bfloat16)


def stats_kernel(dims, images, pos_dev, *refs):
    z_low, z_high, pos_low, pos_high = dims
    blocks = pos_high * z_low * CORES
    in_refs = refs[:blocks]
    mean_hbm, cov_hbm, held, mean_ref, cov_ref, turn_ref, sems = refs[blocks:]
    _, z, core, _, _ = coordinates(lax.axis_index("dp"), lax.axis_index("pos"), (z_low, pos_low))
    for source, ref in enumerate(in_refs):
        pos_step, z_step, core_step = (
            source // (z_low * CORES),
            source // CORES % z_low,
            source % CORES,
        )
        owner = (shift(z, z_low, z_step, -1) * pos_high + pos_step) * CORES + (core ^ core_step)
        held[owner] = ref[...].astype(jnp.float32).reshape(pos_dev, images, LANES)
    everyone = blocks * images
    live = jnp.broadcast_to(
        held[:, 0].reshape(everyone, LANES)[:, CH : CH + 1], (everyone, LANES)
    )
    total = jnp.sum(live, axis=0, keepdims=True)
    factor = 1.0 / (total - 1.0)
    tall = turn_ref.shape[1] // PITCH
    diagonal = lax.broadcasted_iota(jnp.int32, (tall, LANES), 0) == lax.broadcasted_iota(
        jnp.int32, (tall, LANES), 1
    )
    ridge = jnp.where(diagonal, 0.01, 0.0)
    groups = pos_dev // ROWS

    def out(group):
        return pltpu.make_async_copy(
            cov_ref.at[group],
            cov_hbm.at[:, pl.ds(pl.multiple_of(group * ROWS, ROWS), ROWS), :],
            sems.at[group],
        )

    def one_group(group, _):
        for row in range(ROWS):
            position = group * ROWS + row
            samples = held[:, position].reshape(everyone, LANES)
            mean = jnp.sum(samples, axis=0, keepdims=True) / total
            mean_ref[pl.ds(position, 1), :] = mean[:, :CH]
            centered = samples - mean * live
            high = centered.astype(jnp.bfloat16)
            low = (centered - high.astype(jnp.float32)).astype(jnp.bfloat16)
            sums = lax.dot_general(
                jnp.concatenate([high, high, low], axis=0),
                jnp.concatenate([high, low, high], axis=0),
                (((0,), (0,)), ((), ())),
                preferred_element_type=jnp.float32,
            )
            turn_ref[group, pl.ds(row, tall, stride=PITCH), :] = sums[:tall] * factor + ridge
        for channel in range(CH):
            cov_ref[group, channel] = turn_ref[group, pl.ds(channel * PITCH, ROWS), :CH]
        out(group).start()
        return 0

    if everyone > 256:
        lax.fori_loop(0, groups, one_group, 0)
    else:
        for group in range(groups):
            one_group(group, 0)
    mean_out = pltpu.make_async_copy(mean_ref, mean_hbm, sems.at[groups])
    mean_out.start()
    for group in range(groups):
        out(group).wait()
    mean_out.wait()


def on_device(features, counts, channel_order):
    slots, positions, channels = features.shape
    groups, dp = lax.axis_size("pos"), lax.axis_size("dp")
    depth = dp // CORES
    pos_low, pos_high = halves(groups)
    z_low, z_high = halves(depth)
    dims = (z_low, z_high, pos_low, pos_high)
    pos_dev = positions // groups
    images = pos_low * z_high * slots
    wire = jnp.bfloat16
    vmem = pl.BlockSpec(memory_space=pltpu.VMEM)
    hbm = pl.BlockSpec(memory_space=pltpu.HBM)

    def send(block, pos_low_step=0, pos_high_step=0, z_low_step=0, z_high_step=0, core_step=0):
        pairs = []
        for d in range(dp):
            for p in range(groups):
                zh, zl, core, ph, pl_ = coordinates(d, p, (z_low, pos_low))
                z = shift(zh, z_high, z_high_step) * z_low + shift(zl, z_low, z_low_step)
                q = shift(ph, pos_high, pos_high_step) * pos_low + shift(pl_, pos_low, pos_low_step)
                pairs.append((d * groups + p, (z * CORES + (core ^ core_step)) * groups + q))
        return lax.ppermute(block, ("dp", "pos"), pairs)

    half = pos_high * slots * pos_dev
    parts = pl.pallas_call(
        functools.partial(select_kernel, (pos_low, pos_high), pos_dev),
        out_shape=[jax.ShapeDtypeStruct((half, LANES), wire)] * pos_low,
        in_specs=[hbm] * 3,
        out_specs=[vmem] * pos_low,
        scratch_shapes=[
            pltpu.VMEM((slots, channels, positions), wire),
            pltpu.SMEM((1,), jnp.int32),
            pltpu.VMEM((channels,), jnp.int32),
            pltpu.VMEM((slots, positions, LANES), jnp.float32),
            pltpu.SemaphoreType.DMA((3,)),
        ],
        compiler_params=pltpu.CompilerParams(vmem_limit_bytes=16 * MIB),
    )(
        pltpu.with_memory_space_constraint(jnp.transpose(features, (0, 2, 1)), pltpu.HBM),
        counts,
        pltpu.with_memory_space_constraint(channel_order, pltpu.HBM),
    )

    got = {(0, 0): parts[0]}
    for step in far_first(pos_low, z_high):
        got[step] = send(parts[step[0]], pos_low_step=step[0], z_high_step=step[1])

    owns = pl.pallas_call(
        functools.partial(merge_kernel, dims, slots, pos_dev),
        out_shape=[jax.ShapeDtypeStruct((pos_dev * images, LANES), wire)] * pos_high,
        in_specs=[vmem] * (pos_low * z_high),
        out_specs=[vmem] * pos_high,
        scratch_shapes=[pltpu.VMEM((pos_high, pos_dev * images, LANES), jnp.float32)],
        compiler_params=pltpu.CompilerParams(vmem_limit_bytes=32 * MIB),
    )(*(got[p, z] for p in range(pos_low) for z in range(z_high)))

    near = {(0, 0): owns[0]}
    for step in far_first(pos_high, z_low):
        near[step] = send(owns[step[0]], pos_high_step=step[0], z_low_step=step[1])
    arrays = []
    for p in range(pos_high):
        for z in range(z_low):
            arrays += [near[p, z], send(near[p, z], core_step=1)]

    tall = -(-CH // ROWS) * ROWS
    mean, covariance = pl.pallas_call(
        functools.partial(stats_kernel, dims, images, pos_dev),
        out_shape=[
            jax.ShapeDtypeStruct((pos_dev, CH), jnp.float32),
            jax.ShapeDtypeStruct((CH, pos_dev, CH), jnp.float32),
        ],
        in_specs=[vmem] * len(arrays),
        out_specs=[hbm, hbm],
        scratch_shapes=[
            pltpu.VMEM((len(arrays), pos_dev, images, LANES), jnp.float32),
            pltpu.VMEM((pos_dev, CH), jnp.float32),
            pltpu.VMEM((pos_dev // ROWS, CH, ROWS, CH), jnp.float32),
            pltpu.VMEM((pos_dev // ROWS, tall * PITCH, LANES), jnp.float32),
            pltpu.SemaphoreType.DMA((pos_dev // ROWS + 1,)),
        ],
        compiler_params=pltpu.CompilerParams(vmem_limit_bytes=48 * MIB),
    )(*arrays)
    return mean, jnp.transpose(covariance, (1, 0, 2))


def solution(mesh):
    in_specs = (P(("dp", "pos"), None, None), P(("dp", "pos")), P())
    out_specs = (P("pos", None), P("pos", None, None))
    return jax.shard_map(
        on_device, mesh=mesh, in_specs=in_specs, out_specs=out_specs, check_vma=False
    )
```

time: 130 us -> 23 us (0.18)
  waiting for transfers between devices: 65 us -> 9.22 us
  blocking collectives: 27.4 us -> 0 us
  between operations: 15.4 us -> 1.3 us
  other arithmetic: 4.59 us -> 0 us
  matrix products: 4.57 us -> 0 us
  local copies, waits for them, and re-layouts: 4.13 us -> 0 us
  Pallas kernels: 0 us -> 3.06 us
    psum x1 -> x0, waiting for transfers between devices: 58.5 us -> none  [on_device(): summed = lax.psum(own_term, 'dp')]
    psum x1 -> x0, blocking collectives: 27.4 us -> none  [common_mean(): total_count, total_sums = lax.psum((group_count, group_sums), 'dp')]
    ppermute x0 -> x10, waiting for transfers between devices: none -> 9.22 us  [send(): return lax.ppermute(block, ('dp', 'pos'), pairs)]
    ppermute x0 -> x10, starting transfers between devices: none -> 9.21 us  [send(): return lax.ppermute(block, ('dp', 'pos'), pairs)]
    all_to_all x2 -> x0, starting transfers between devices: 8.44 us -> none  [the longest x1 5.16 us: on_device(): lax.all_to_all(owned_wire, 'pos', split_axis=1, concat_axis=0, tiled=True)]
    all_to_all x2 -> x0, waiting for transfers between devices: 6.49 us -> none  [the longest x1 3.88 us: on_device(): lax.all_to_all(packed, 'pos', split_axis=1, concat_axis=0, tiled=True)]
    dot_general x2 -> x0, matrix products: 4.57 us -> none  [the longest x1 4.36 us: local_stats(): jnp.einsum('gpc,gpd->pcd', centered, centered, precision=lax.Precision.HI...]
    pallas_call x0 -> x3, Pallas kernels: none -> 3.06 us  [the longest x1 1.83 us: on_device(): pl.pallas_call(functools.partial(stats_kernel, dims, images, pos_dev), ou...]
  transfers between devices with their start and end apart: 3 -> 10, of which waited for: 3 -> 7; matrix products, arithmetic and copies ran while one was open for 2% -> 0% of each run, Pallas kernels for 0% -> 0%
where the time goes in v2:
time: 23 us; the launch traced here: 22.8 us
  waiting for transfers between devices  9.22 us (40%)
  starting transfers between devices  9.21 us (40%)
  Pallas kernels  3.06 us (13%)
  between operations  1.3 us (6%)
    ppermute x10, waiting for transfers between devices, send(): return lax.ppermute(block, ('dp', 'pos'), pairs)  9.22 us
    ppermute x10, starting transfers between devices, send(): return lax.ppermute(block, ('dp', 'pos'), pairs)  9.21 us
    pallas_call x1, Pallas kernels, on_device(): pl.pallas_call(functools.partial(stats_kernel, dims, images, pos_dev), ou...  1.83 us
    pallas_call x1, Pallas kernels, on_device(): pl.pallas_call(functools.partial(select_kernel, (pos_low, pos_high), pos_...  1.17 us
  transfers between devices with their start and end apart: 10, of which 7 were waited for; matrix products, arithmetic and copies ran while one was open for 0% of the time, Pallas kernels for 0%

profile of v2, /device:TPU:0, one launch (start us, length us, event | category | flops | bytes accessed | tf_op | source)
XLA Modules:
  0.0 22.8 jit_solution(101108736712844591)
XLA Ops:
  1.3 1.2 %shard_map.50 = (bf16[128,128]{1,0:T(8,128)(2,1)S(1)}, bf16[128,128]{1,0:T(8,128)(2,1)S(1)}) custom-call(bf16[2,224,128]{2,1,0:T(8,128)(2,1)} %bitcast.2, s32[1]{0:T(128)S(6)} %copy.5.counts_hbm, s32[224]{0:T(256)} %order_hbm.1), custom_call_target="tpu_custom_call" | custom-call | tf_op jit(solution)/shard_map/pallas_call | solution.py:187
  2.4 4.1 %collective-permute-start = (bf16[128,128]{1,0:T(8,128)(2,1)S(1)}, bf16[128,128]{1,0:T(8,128)(2,1)S(1)}, u32[]{:S(2)}, u32[]{:S(2)}) collective-permute-start(bf16[128,128]{1,0:T(8,128)(2,1)S(1)} %get-tuple-element.8.refs_0_), channel_id=1, source_target_pairs={{0,16},{1,17},{2,18},{3,19},{4,20},{5,21},{6,22},{7,23},{8,24},{9,... | collective-permute-start | bytes 98312 | tf_op jit(solution)/shard_map/ppermute | solution.py:184
  6.6 1.3 %collective-permute-start.2 = (bf16[128,128]{1,0:T(8,128)(2,1)S(1)}, bf16[128,128]{1,0:T(8,128)(2,1)S(1)}, u32[]{:S(2)}, u32[]{:S(2)}) collective-permute-start(bf16[128,128]{1,0:T(8,128)(2,1)S(1)} %get-tuple-element.9), channel_id=1, source_target_pairs={{0,17},{1,16},{2,19},{3,18},{4,21},{5,20},{6,23},{7,22},{8,25},{9,... | collective-permute-start | bytes 98312 | tf_op jit(solution)/shard_map/ppermute | solution.py:184
  7.8 0.3 %collective-permute-start.1 = (bf16[128,128]{1,0:T(8,128)(2,1)S(1)}, bf16[128,128]{1,0:T(8,128)(2,1)S(1)}, u32[]{:S(2)}, u32[]{:S(2)}) collective-permute-start(bf16[128,128]{1,0:T(8,128)(2,1)S(1)} %get-tuple-element.9), channel_id=1, source_target_pairs={{0,1},{1,0},{2,3},{3,2},{4,5},{5,4},{6,7},{7,6},{8,9},{9,8},{10,11... | collective-permute-start | bytes 98312 | tf_op jit(solution)/shard_map/ppermute | solution.py:184
  8.1 0.7 %collective-permute-done.refs_1_ = bf16[128,128]{1,0:T(8,128)(2,1)S(1)} collective-permute-done((bf16[128,128]{1,0:T(8,128)(2,1)S(1)}, bf16[128,128]{1,0:T(8,128)(2,1)S(1)}, u32[]{:S(2)}, u32[]{:S(2)}) %collective-permute-start) | collective-permute-done | bytes 32800 | tf_op jit(solution)/shard_map/ppermute | solution.py:184
  8.8 3.5 %collective-permute-done.2.refs_3_ = bf16[128,128]{1,0:T(8,128)(2,1)S(1)} collective-permute-done((bf16[128,128]{1,0:T(8,128)(2,1)S(1)}, bf16[128,128]{1,0:T(8,128)(2,1)S(1)}, u32[]{:S(2)}, u32[]{:S(2)}) %collective-permute-start.2) | collective-permute-done | bytes 32800 | tf_op jit(solution)/shard_map/ppermute | solution.py:184
  12.3 0.0 collective-permute-done.1.refs_2_
  12.3 0.1 shard_map.51
  12.3 2.6 %collective-permute-start.8 = (bf16[256,128]{1,0:T(8,128)(2,1)S(1)}, bf16[256,128]{1,0:T(8,128)(2,1)S(1)}, u32[]{:S(2)}, u32[]{:S(2)}) collective-permute-start(bf16[256,128]{1,0:T(8,128)(2,1)S(1)} %get-tuple-element.11), channel_id=1, source_target_pairs={{0,10},{1,11},{2,8},{3,9},{4,14},{5,15},{6,12},{7,13},{8,2},{9,3},... | collective-permute-start | bytes 196616 | tf_op jit(solution)/shard_map/ppermute | solution.py:184
  14.9 0.5 %collective-permute-start.6 = (bf16[256,128]{1,0:T(8,128)(2,1)S(1)}, bf16[256,128]{1,0:T(8,128)(2,1)S(1)}, u32[]{:S(2)}, u32[]{:S(2)}) collective-permute-start(bf16[256,128]{1,0:T(8,128)(2,1)S(1)} %get-tuple-element.11), channel_id=1, source_target_pairs={{0,2},{1,3},{2,0},{3,1},{4,6},{5,7},{6,4},{7,5},{8,10},{9,11},{10,... | collective-permute-start | bytes 196616 | tf_op jit(solution)/shard_map/ppermute | solution.py:184
  15.4 0.4 %collective-permute-start.4 = (bf16[256,128]{1,0:T(8,128)(2,1)S(1)}, bf16[256,128]{1,0:T(8,128)(2,1)S(1)}, u32[]{:S(2)}, u32[]{:S(2)}) collective-permute-start(bf16[256,128]{1,0:T(8,128)(2,1)S(1)} %get-tuple-element.10.refs_0_), channel_id=1, source_target_pairs={{0,8},{1,9},{2,10},{3,11},{4,12},{5,13},{6,14},{7,15},{8,0},{9,1},... | collective-permute-start | bytes 196616 | tf_op jit(solution)/shard_map/ppermute | solution.py:184
  15.9 0.0 collective-permute-start.3
  15.9 2.3 %collective-permute-done.8.refs_6_ = bf16[256,128]{1,0:T(8,128)(2,1)S(1)} collective-permute-done((bf16[256,128]{1,0:T(8,128)(2,1)S(1)}, bf16[256,128]{1,0:T(8,128)(2,1)S(1)}, u32[]{:S(2)}, u32[]{:S(2)}) %collective-permute-start.8) | collective-permute-done | bytes 65568 | tf_op jit(solution)/shard_map/ppermute | solution.py:184
  18.2 0.0 collective-permute-start.9
  18.2 1.0 %collective-permute-done.6.refs_4_ = bf16[256,128]{1,0:T(8,128)(2,1)S(1)} collective-permute-done((bf16[256,128]{1,0:T(8,128)(2,1)S(1)}, bf16[256,128]{1,0:T(8,128)(2,1)S(1)}, u32[]{:S(2)}, u32[]{:S(2)}) %collective-permute-start.6) | collective-permute-done | bytes 65568 | tf_op jit(solution)/shard_map/ppermute | solution.py:184
  19.2 0.0 collective-permute-start.7
  19.2 0.5 %collective-permute-done.4.refs_2_ = bf16[256,128]{1,0:T(8,128)(2,1)S(1)} collective-permute-done((bf16[256,128]{1,0:T(8,128)(2,1)S(1)}, bf16[256,128]{1,0:T(8,128)(2,1)S(1)}, u32[]{:S(2)}, u32[]{:S(2)}) %collective-permute-start.4) | collective-permute-done | bytes 65568 | tf_op jit(solution)/shard_map/ppermute | solution.py:184
  19.7 0.0 collective-permute-start.5
  19.7 0.0 collective-permute-done.3.refs_1_
  19.7 0.0 collective-permute-done.9.refs_7_
  19.7 0.7 %collective-permute-done.7.refs_5_ = bf16[256,128]{1,0:T(8,128)(2,1)S(1)} collective-permute-done((bf16[256,128]{1,0:T(8,128)(2,1)S(1)}, bf16[256,128]{1,0:T(8,128)(2,1)S(1)}, u32[]{:S(2)}, u32[]{:S(2)}) %collective-permute-start.7) | collective-permute-done | bytes 65568 | tf_op jit(solution)/shard_map/ppermute | solution.py:184
  20.5 0.5 %collective-permute-done.5.refs_3_ = bf16[256,128]{1,0:T(8,128)(2,1)S(1)} collective-permute-done((bf16[256,128]{1,0:T(8,128)(2,1)S(1)}, bf16[256,128]{1,0:T(8,128)(2,1)S(1)}, u32[]{:S(2)}, u32[]{:S(2)}) %collective-permute-start.5) | collective-permute-done | bytes 65568 | tf_op jit(solution)/shard_map/ppermute | solution.py:184
  21.0 1.8 %shard_map.52 = (f32[32,100]{1,0:T(8,128)}, f32[100,32,100]{2,1,0:T(8,128)}) custom-call(bf16[256,128]{1,0:T(8,128)(2,1)S(1)} %get-tuple-element.10.refs_0_, bf16[256,128]{1,0:T(8,128)(2,1)S(1)} %collective-permute-done.3.refs_1_, bf16[256,128]{1,0:T(8,128)(2,1)S(1)} %collective-permute-done.4.refs_2_, bf16[256,128]{1,0:T(8,128)(2,1)S(1)} %collective-permute-done.5.refs_3_, ...), custom_call_target="tpu_custom_call" | custom-call | tf_op jit(solution)/shard_map/pallas_call | solution.py:228
Async XLA Ops:
  2.4 6.3 %collective-permute-start = (bf16[128,128]{1,0:T(8,128)(2,1)S(1)}, bf16[128,128]{1,0:T(8,128)(2,1)S(1)}, u32[]{:S(2)}, u32[]{:S(2)}) collective-permute-start(bf16[128,128]{1,0:T(8,128)(2,1)S(1)} %get-tuple-element.8.refs_0_), channel_id=1, source_target_pairs={{0,16},{1,17},{2,18},{3,19},{4,20},{5,21},{6,22},{7,23},{8,24},{9,... | collective-permute-start | bytes 98312 | tf_op jit(solution)/shard_map/ppermute | solution.py:184
  6.6 5.7 %collective-permute-start.2 = (bf16[128,128]{1,0:T(8,128)(2,1)S(1)}, bf16[128,128]{1,0:T(8,128)(2,1)S(1)}, u32[]{:S(2)}, u32[]{:S(2)}) collective-permute-start(bf16[128,128]{1,0:T(8,128)(2,1)S(1)} %get-tuple-element.9), channel_id=1, source_target_pairs={{0,17},{1,16},{2,19},{3,18},{4,21},{5,20},{6,23},{7,22},{8,25},{9,... | collective-permute-start | bytes 98312 | tf_op jit(solution)/shard_map/ppermute | solution.py:184
  7.8 4.5 %collective-permute-start.1 = (bf16[128,128]{1,0:T(8,128)(2,1)S(1)}, bf16[128,128]{1,0:T(8,128)(2,1)S(1)}, u32[]{:S(2)}, u32[]{:S(2)}) collective-permute-start(bf16[128,128]{1,0:T(8,128)(2,1)S(1)} %get-tuple-element.9), channel_id=1, source_target_pairs={{0,1},{1,0},{2,3},{3,2},{4,5},{5,4},{6,7},{7,6},{8,9},{9,8},{10,11... | collective-permute-start | bytes 98312 | tf_op jit(solution)/shard_map/ppermute | solution.py:184
  12.3 5.9 %collective-permute-start.8 = (bf16[256,128]{1,0:T(8,128)(2,1)S(1)}, bf16[256,128]{1,0:T(8,128)(2,1)S(1)}, u32[]{:S(2)}, u32[]{:S(2)}) collective-permute-start(bf16[256,128]{1,0:T(8,128)(2,1)S(1)} %get-tuple-element.11), channel_id=1, source_target_pairs={{0,10},{1,11},{2,8},{3,9},{4,14},{5,15},{6,12},{7,13},{8,2},{9,3},... | collective-permute-start | bytes 196616 | tf_op jit(solution)/shard_map/ppermute | solution.py:184
  14.9 4.3 %collective-permute-start.6 = (bf16[256,128]{1,0:T(8,128)(2,1)S(1)}, bf16[256,128]{1,0:T(8,128)(2,1)S(1)}, u32[]{:S(2)}, u32[]{:S(2)}) collective-permute-start(bf16[256,128]{1,0:T(8,128)(2,1)S(1)} %get-tuple-element.11), channel_id=1, source_target_pairs={{0,2},{1,3},{2,0},{3,1},{4,6},{5,7},{6,4},{7,5},{8,10},{9,11},{10,... | collective-permute-start | bytes 196616 | tf_op jit(solution)/shard_map/ppermute | solution.py:184
  15.4 4.3 %collective-permute-start.4 = (bf16[256,128]{1,0:T(8,128)(2,1)S(1)}, bf16[256,128]{1,0:T(8,128)(2,1)S(1)}, u32[]{:S(2)}, u32[]{:S(2)}) collective-permute-start(bf16[256,128]{1,0:T(8,128)(2,1)S(1)} %get-tuple-element.10.refs_0_), channel_id=1, source_target_pairs={{0,8},{1,9},{2,10},{3,11},{4,12},{5,13},{6,14},{7,15},{8,0},{9,1},... | collective-permute-start | bytes 196616 | tf_op jit(solution)/shard_map/ppermute | solution.py:184
  15.9 3.8 %collective-permute-start.3 = (bf16[256,128]{1,0:T(8,128)(2,1)S(1)}, bf16[256,128]{1,0:T(8,128)(2,1)S(1)}, u32[]{:S(2)}, u32[]{:S(2)}) collective-permute-start(bf16[256,128]{1,0:T(8,128)(2,1)S(1)} %get-tuple-element.10.refs_0_), channel_id=1, source_target_pairs={{0,4},{1,5},{2,6},{3,7},{4,0},{5,1},{6,2},{7,3},{8,12},{9,13},{10,... | collective-permute-start | bytes 196616 | tf_op jit(solution)/shard_map/ppermute | solution.py:184
  18.2 1.5 %collective-permute-start.9 = (bf16[256,128]{1,0:T(8,128)(2,1)S(1)}, bf16[256,128]{1,0:T(8,128)(2,1)S(1)}, u32[]{:S(2)}, u32[]{:S(2)}) collective-permute-start(bf16[256,128]{1,0:T(8,128)(2,1)S(1)} %collective-permute-done.8.refs_6_), channel_id=1, source_target_pairs={{0,4},{1,5},{2,6},{3,7},{4,0},{5,1},{6,2},{7,3},{8,12},{9,13},{10,... | collective-permute-start | bytes 196616 | tf_op jit(solution)/shard_map/ppermute | solution.py:184
  19.2 1.3 %collective-permute-start.7 = (bf16[256,128]{1,0:T(8,128)(2,1)S(1)}, bf16[256,128]{1,0:T(8,128)(2,1)S(1)}, u32[]{:S(2)}, u32[]{:S(2)}) collective-permute-start(bf16[256,128]{1,0:T(8,128)(2,1)S(1)} %collective-permute-done.6.refs_4_), channel_id=1, source_target_pairs={{0,4},{1,5},{2,6},{3,7},{4,0},{5,1},{6,2},{7,3},{8,12},{9,13},{10,... | collective-permute-start | bytes 196616 | tf_op jit(solution)/shard_map/ppermute | solution.py:184
  19.7 1.3 %collective-permute-start.5 = (bf16[256,128]{1,0:T(8,128)(2,1)S(1)}, bf16[256,128]{1,0:T(8,128)(2,1)S(1)}, u32[]{:S(2)}, u32[]{:S(2)}) collective-permute-start(bf16[256,128]{1,0:T(8,128)(2,1)S(1)} %collective-permute-done.4.refs_2_), channel_id=1, source_target_pairs={{0,4},{1,5},{2,6},{3,7},{4,0},{5,1},{6,2},{7,3},{8,12},{9,13},{10,... | collective-permute-start | bytes 196616 | tf_op jit(solution)/shard_map/ppermute | solution.py:184

commit v3 on v2

--- a/solution.py
+++ b/solution.py
@@ -98,15 +98,19 @@
     blocks = pos_high * z_low * CORES
     in_refs = refs[:blocks]
     mean_hbm, cov_hbm, held, mean_ref, cov_ref, turn_ref, sems = refs[blocks:]
-    _, z, core, _, _ = coordinates(lax.axis_index("dp"), lax.axis_index("pos"), (z_low, pos_low))
-    for source, ref in enumerate(in_refs):
-        pos_step, z_step, core_step = (
-            source // (z_low * CORES),
-            source // CORES % z_low,
-            source % CORES,
-        )
-        owner = (shift(z, z_low, z_step, -1) * pos_high + pos_step) * CORES + (core ^ core_step)
-        held[owner] = ref[...].astype(jnp.float32).reshape(pos_dev, images, LANES)
+    z_top, z, core, _, _ = coordinates(lax.axis_index("dp"), lax.axis_index("pos"), (z_low, pos_low))
+    slot = lax.broadcasted_iota(jnp.int32, (1, images, LANES), 1)
+    kept = slot // (images // (z_high * pos_low)) == z_top * pos_low
+    for pair in range(blocks // CORES):
+        pos_step, z_step = pair // z_low, pair % z_low
+        base = (shift(z, z_low, z_step, -1) * pos_high + pos_step) * CORES
+        near = core if pair == 0 else 1 - core
+        first, second = (
+            in_refs[pair * CORES + i][...].astype(jnp.float32).reshape(pos_dev, images, LANES)
+            for i in range(CORES)
+        )
+        held[base + near] = jnp.where(kept, first, second)
+        held[base + 1 - near] = jnp.where(kept, second, first)
     everyone = blocks * images
     live = jnp.broadcast_to(
         held[:, 0].reshape(everyone, LANES)[:, CH : CH + 1], (everyone, LANES)
@@ -205,7 +209,7 @@
 
     got = {(0, 0): parts[0]}
     for step in far_first(pos_low, z_high):
-        got[step] = send(parts[step[0]], pos_low_step=step[0], z_high_step=step[1])
+        got[step] = send(parts[step[0]], pos_low_step=step[0], z_high_step=step[1], core_step=1)
 
     owns = pl.pallas_call(
         functools.partial(merge_kernel, dims, slots, pos_dev),
@@ -218,7 +222,7 @@
 
     near = {(0, 0): owns[0]}
     for step in far_first(pos_high, z_low):
-        near[step] = send(owns[step[0]], pos_high_step=step[0], z_low_step=step[1])
+        near[step] = send(owns[step[0]], pos_high_step=step[0], z_low_step=step[1], core_step=1)
     arrays = []
     for p in range(pos_high):
         for z in range(z_low):

time: 23 us -> 21.8 us (0.948)
  waiting for transfers between devices: 9.22 us -> 7 us
  starting transfers between devices: 9.21 us -> 10.2 us
    ppermute x10, waiting for transfers between devices: 9.22 us -> 7 us  [send(): return lax.ppermute(block, ('dp', 'pos'), pairs)]
    ppermute x10, starting transfers between devices: 9.21 us -> 10.2 us  [send(): return lax.ppermute(block, ('dp', 'pos'), pairs)]
  transfers between devices with their start and end apart: 10 -> 10, of which waited for: 7 -> 5; matrix products, arithmetic and copies ran while one was open for 0% -> 0% of each run, Pallas kernels for 0% -> 0%
where the time goes in v3:
time: 21.8 us; the launch traced here: 21.6 us
  starting transfers between devices  10.2 us (47%)
  waiting for transfers between devices  7 us (32%)
  Pallas kernels  3.09 us (14%)
  between operations  1.3 us (6%)
    ppermute x10, starting transfers between devices, send(): return lax.ppermute(block, ('dp', 'pos'), pairs)  10.2 us
    ppermute x10, waiting for transfers between devices, send(): return lax.ppermute(block, ('dp', 'pos'), pairs)  7 us
    pallas_call x1, Pallas kernels, on_device(): pl.pallas_call(functools.partial(stats_kernel, dims, images, pos_dev), ou...  1.87 us
    pallas_call x1, Pallas kernels, on_device(): pl.pallas_call(functools.partial(select_kernel, (pos_low, pos_high), pos_...  1.17 us
  transfers between devices with their start and end apart: 10, of which 5 were waited for; matrix products, arithmetic and copies ran while one was open for 0% of the time, Pallas kernels for 0%

profile of v3, /device:TPU:0, one launch (start us, length us, event | category | flops | bytes accessed | tf_op | source)
XLA Modules:
  0.0 21.6 jit_solution(9639346806152549610)
XLA Ops:
  1.3 1.2 %shard_map.50 = (bf16[128,128]{1,0:T(8,128)(2,1)S(1)}, bf16[128,128]{1,0:T(8,128)(2,1)S(1)}) custom-call(bf16[2,224,128]{2,1,0:T(8,128)(2,1)} %bitcast.2, s32[1]{0:T(128)S(6)} %copy.5.counts_hbm, s32[224]{0:T(256)} %order_hbm.1), custom_call_target="tpu_custom_call" | custom-call | tf_op jit(solution)/shard_map/pallas_call | solution.py:191
  2.4 3.5 %collective-permute-start = (bf16[128,128]{1,0:T(8,128)(2,1)S(1)}, bf16[128,128]{1,0:T(8,128)(2,1)S(1)}, u32[]{:S(2)}, u32[]{:S(2)}) collective-permute-start(bf16[128,128]{1,0:T(8,128)(2,1)S(1)} %get-tuple-element.8.refs_0_), channel_id=1, source_target_pairs={{0,20},{1,21},{2,22},{3,23},{4,16},{5,17},{6,18},{7,19},{8,28},{9,... | collective-permute-start | bytes 98312 | tf_op jit(solution)/shard_map/ppermute | solution.py:188
  6.0 1.5 %collective-permute-start.2 = (bf16[128,128]{1,0:T(8,128)(2,1)S(1)}, bf16[128,128]{1,0:T(8,128)(2,1)S(1)}, u32[]{:S(2)}, u32[]{:S(2)}) collective-permute-start(bf16[128,128]{1,0:T(8,128)(2,1)S(1)} %get-tuple-element.9), channel_id=1, source_target_pairs={{0,21},{1,20},{2,23},{3,22},{4,17},{5,16},{6,19},{7,18},{8,29},{9,... | collective-permute-start | bytes 98312 | tf_op jit(solution)/shard_map/ppermute | solution.py:188
  7.5 0.3 %collective-permute-start.1 = (bf16[128,128]{1,0:T(8,128)(2,1)S(1)}, bf16[128,128]{1,0:T(8,128)(2,1)S(1)}, u32[]{:S(2)}, u32[]{:S(2)}) collective-permute-start(bf16[128,128]{1,0:T(8,128)(2,1)S(1)} %get-tuple-element.9), channel_id=1, source_target_pairs={{0,5},{1,4},{2,7},{3,6},{4,1},{5,0},{6,3},{7,2},{8,13},{9,12},{10,... | collective-permute-start | bytes 98312 | tf_op jit(solution)/shard_map/ppermute | solution.py:188
  7.8 0.0 collective-permute-done.refs_1_
  7.8 3.4 %collective-permute-done.2.refs_3_ = bf16[128,128]{1,0:T(8,128)(2,1)S(1)} collective-permute-done((bf16[128,128]{1,0:T(8,128)(2,1)S(1)}, bf16[128,128]{1,0:T(8,128)(2,1)S(1)}, u32[]{:S(2)}, u32[]{:S(2)}) %collective-permute-start.2) | collective-permute-done | bytes 32800 | tf_op jit(solution)/shard_map/ppermute | solution.py:188
  11.2 0.0 collective-permute-done.1.refs_2_
  11.3 0.1 shard_map.51
  11.3 2.8 %collective-permute-start.8 = (bf16[256,128]{1,0:T(8,128)(2,1)S(1)}, bf16[256,128]{1,0:T(8,128)(2,1)S(1)}, u32[]{:S(2)}, u32[]{:S(2)}) collective-permute-start(bf16[256,128]{1,0:T(8,128)(2,1)S(1)} %get-tuple-element.11), channel_id=1, source_target_pairs={{0,14},{1,15},{2,12},{3,13},{4,10},{5,11},{6,8},{7,9},{8,6},{9,7},... | collective-permute-start | bytes 196616 | tf_op jit(solution)/shard_map/ppermute | solution.py:188
  14.1 0.1 collective-permute-start.6
  14.2 0.9 %collective-permute-start.4 = (bf16[256,128]{1,0:T(8,128)(2,1)S(1)}, bf16[256,128]{1,0:T(8,128)(2,1)S(1)}, u32[]{:S(2)}, u32[]{:S(2)}) collective-permute-start(bf16[256,128]{1,0:T(8,128)(2,1)S(1)} %get-tuple-element.10.refs_0_), channel_id=1, source_target_pairs={{0,12},{1,13},{2,14},{3,15},{4,8},{5,9},{6,10},{7,11},{8,4},{9,5},... | collective-permute-start | bytes 196616 | tf_op jit(solution)/shard_map/ppermute | solution.py:188
  15.1 0.0 collective-permute-start.3
  15.1 1.2 %collective-permute-done.8.refs_6_ = bf16[256,128]{1,0:T(8,128)(2,1)S(1)} collective-permute-done((bf16[256,128]{1,0:T(8,128)(2,1)S(1)}, bf16[256,128]{1,0:T(8,128)(2,1)S(1)}, u32[]{:S(2)}, u32[]{:S(2)}) %collective-permute-start.8) | collective-permute-done | bytes 65568 | tf_op jit(solution)/shard_map/ppermute | solution.py:188
  16.3 0.5 %collective-permute-start.9 = (bf16[256,128]{1,0:T(8,128)(2,1)S(1)}, bf16[256,128]{1,0:T(8,128)(2,1)S(1)}, u32[]{:S(2)}, u32[]{:S(2)}) collective-permute-start(bf16[256,128]{1,0:T(8,128)(2,1)S(1)} %collective-permute-done.8.refs_6_), channel_id=1, source_target_pairs={{0,4},{1,5},{2,6},{3,7},{4,0},{5,1},{6,2},{7,3},{8,12},{9,13},{10,... | collective-permute-start | bytes 196616 | tf_op jit(solution)/shard_map/ppermute | solution.py:188
  16.9 1.4 %collective-permute-done.6.refs_4_ = bf16[256,128]{1,0:T(8,128)(2,1)S(1)} collective-permute-done((bf16[256,128]{1,0:T(8,128)(2,1)S(1)}, bf16[256,128]{1,0:T(8,128)(2,1)S(1)}, u32[]{:S(2)}, u32[]{:S(2)}) %collective-permute-start.6) | collective-permute-done | bytes 65568 | tf_op jit(solution)/shard_map/ppermute | solution.py:188
  18.3 0.1 collective-permute-start.7
  18.4 0.0 collective-permute-done.4.refs_2_
  18.4 0.4 %collective-permute-start.5 = (bf16[256,128]{1,0:T(8,128)(2,1)S(1)}, bf16[256,128]{1,0:T(8,128)(2,1)S(1)}, u32[]{:S(2)}, u32[]{:S(2)}) collective-permute-start(bf16[256,128]{1,0:T(8,128)(2,1)S(1)} %collective-permute-done.4.refs_2_), channel_id=1, source_target_pairs={{0,4},{1,5},{2,6},{3,7},{4,0},{5,1},{6,2},{7,3},{8,12},{9,13},{10,... | collective-permute-start | bytes 196616 | tf_op jit(solution)/shard_map/ppermute | solution.py:188
  18.8 0.0 collective-permute-done.3.refs_1_
  18.8 0.0 collective-permute-done.9.refs_7_
  18.8 0.7 %collective-permute-done.7.refs_5_ = bf16[256,128]{1,0:T(8,128)(2,1)S(1)} collective-permute-done((bf16[256,128]{1,0:T(8,128)(2,1)S(1)}, bf16[256,128]{1,0:T(8,128)(2,1)S(1)}, u32[]{:S(2)}, u32[]{:S(2)}) %collective-permute-start.7) | collective-permute-done | bytes 65568 | tf_op jit(solution)/shard_map/ppermute | solution.py:188
  19.6 0.2 collective-permute-done.5.refs_3_
  19.7 1.9 %shard_map.52 = (f32[32,100]{1,0:T(8,128)}, f32[100,32,100]{2,1,0:T(8,128)}) custom-call(bf16[256,128]{1,0:T(8,128)(2,1)S(1)} %get-tuple-element.10.refs_0_, bf16[256,128]{1,0:T(8,128)(2,1)S(1)} %collective-permute-done.3.refs_1_, bf16[256,128]{1,0:T(8,128)(2,1)S(1)} %collective-permute-done.4.refs_2_, bf16[256,128]{1,0:T(8,128)(2,1)S(1)} %collective-permute-done.5.refs_3_, ...), custom_call_target="tpu_custom_call" | custom-call | tf_op jit(solution)/shard_map/pallas_call | solution.py:232
Async XLA Ops:
  2.4 5.4 %collective-permute-start = (bf16[128,128]{1,0:T(8,128)(2,1)S(1)}, bf16[128,128]{1,0:T(8,128)(2,1)S(1)}, u32[]{:S(2)}, u32[]{:S(2)}) collective-permute-start(bf16[128,128]{1,0:T(8,128)(2,1)S(1)} %get-tuple-element.8.refs_0_), channel_id=1, source_target_pairs={{0,20},{1,21},{2,22},{3,23},{4,16},{5,17},{6,18},{7,19},{8,28},{9,... | collective-permute-start | bytes 98312 | tf_op jit(solution)/shard_map/ppermute | solution.py:188
  6.0 5.2 %collective-permute-start.2 = (bf16[128,128]{1,0:T(8,128)(2,1)S(1)}, bf16[128,128]{1,0:T(8,128)(2,1)S(1)}, u32[]{:S(2)}, u32[]{:S(2)}) collective-permute-start(bf16[128,128]{1,0:T(8,128)(2,1)S(1)} %get-tuple-element.9), channel_id=1, source_target_pairs={{0,21},{1,20},{2,23},{3,22},{4,17},{5,16},{6,19},{7,18},{8,29},{9,... | collective-permute-start | bytes 98312 | tf_op jit(solution)/shard_map/ppermute | solution.py:188
  7.5 3.7 %collective-permute-start.1 = (bf16[128,128]{1,0:T(8,128)(2,1)S(1)}, bf16[128,128]{1,0:T(8,128)(2,1)S(1)}, u32[]{:S(2)}, u32[]{:S(2)}) collective-permute-start(bf16[128,128]{1,0:T(8,128)(2,1)S(1)} %get-tuple-element.9), channel_id=1, source_target_pairs={{0,5},{1,4},{2,7},{3,6},{4,1},{5,0},{6,3},{7,2},{8,13},{9,12},{10,... | collective-permute-start | bytes 98312 | tf_op jit(solution)/shard_map/ppermute | solution.py:188
  11.3 5.0 %collective-permute-start.8 = (bf16[256,128]{1,0:T(8,128)(2,1)S(1)}, bf16[256,128]{1,0:T(8,128)(2,1)S(1)}, u32[]{:S(2)}, u32[]{:S(2)}) collective-permute-start(bf16[256,128]{1,0:T(8,128)(2,1)S(1)} %get-tuple-element.11), channel_id=1, source_target_pairs={{0,14},{1,15},{2,12},{3,13},{4,10},{5,11},{6,8},{7,9},{8,6},{9,7},... | collective-permute-start | bytes 196616 | tf_op jit(solution)/shard_map/ppermute | solution.py:188
  14.1 4.2 %collective-permute-start.6 = (bf16[256,128]{1,0:T(8,128)(2,1)S(1)}, bf16[256,128]{1,0:T(8,128)(2,1)S(1)}, u32[]{:S(2)}, u32[]{:S(2)}) collective-permute-start(bf16[256,128]{1,0:T(8,128)(2,1)S(1)} %get-tuple-element.11), channel_id=1, source_target_pairs={{0,6},{1,7},{2,4},{3,5},{4,2},{5,3},{6,0},{7,1},{8,14},{9,15},{10,... | collective-permute-start | bytes 196616 | tf_op jit(solution)/shard_map/ppermute | solution.py:188
  14.2 4.3 %collective-permute-start.4 = (bf16[256,128]{1,0:T(8,128)(2,1)S(1)}, bf16[256,128]{1,0:T(8,128)(2,1)S(1)}, u32[]{:S(2)}, u32[]{:S(2)}) collective-permute-start(bf16[256,128]{1,0:T(8,128)(2,1)S(1)} %get-tuple-element.10.refs_0_), channel_id=1, source_target_pairs={{0,12},{1,13},{2,14},{3,15},{4,8},{5,9},{6,10},{7,11},{8,4},{9,5},... | collective-permute-start | bytes 196616 | tf_op jit(solution)/shard_map/ppermute | solution.py:188
  15.1 3.7 %collective-permute-start.3 = (bf16[256,128]{1,0:T(8,128)(2,1)S(1)}, bf16[256,128]{1,0:T(8,128)(2,1)S(1)}, u32[]{:S(2)}, u32[]{:S(2)}) collective-permute-start(bf16[256,128]{1,0:T(8,128)(2,1)S(1)} %get-tuple-element.10.refs_0_), channel_id=1, source_target_pairs={{0,4},{1,5},{2,6},{3,7},{4,0},{5,1},{6,2},{7,3},{8,12},{9,13},{10,... | collective-permute-start | bytes 196616 | tf_op jit(solution)/shard_map/ppermute | solution.py:188
  16.3 2.5 %collective-permute-start.9 = (bf16[256,128]{1,0:T(8,128)(2,1)S(1)}, bf16[256,128]{1,0:T(8,128)(2,1)S(1)}, u32[]{:S(2)}, u32[]{:S(2)}) collective-permute-start(bf16[256,128]{1,0:T(8,128)(2,1)S(1)} %collective-permute-done.8.refs_6_), channel_id=1, source_target_pairs={{0,4},{1,5},{2,6},{3,7},{4,0},{5,1},{6,2},{7,3},{8,12},{9,13},{10,... | collective-permute-start | bytes 196616 | tf_op jit(solution)/shard_map/ppermute | solution.py:188
  18.3 1.3 %collective-permute-start.7 = (bf16[256,128]{1,0:T(8,128)(2,1)S(1)}, bf16[256,128]{1,0:T(8,128)(2,1)S(1)}, u32[]{:S(2)}, u32[]{:S(2)}) collective-permute-start(bf16[256,128]{1,0:T(8,128)(2,1)S(1)} %collective-permute-done.6.refs_4_), channel_id=1, source_target_pairs={{0,4},{1,5},{2,6},{3,7},{4,0},{5,1},{6,2},{7,3},{8,12},{9,13},{10,... | collective-permute-start | bytes 196616 | tf_op jit(solution)/shard_map/ppermute | solution.py:188
  18.4 1.3 %collective-permute-start.5 = (bf16[256,128]{1,0:T(8,128)(2,1)S(1)}, bf16[256,128]{1,0:T(8,128)(2,1)S(1)}, u32[]{:S(2)}, u32[]{:S(2)}) collective-permute-start(bf16[256,128]{1,0:T(8,128)(2,1)S(1)} %collective-permute-done.4.refs_2_), channel_id=1, source_target_pairs={{0,4},{1,5},{2,6},{3,7},{4,0},{5,1},{6,2},{7,3},{8,12},{9,13},{10,... | collective-permute-start | bytes 196616 | tf_op jit(solution)/shard_map/ppermute | solution.py:188

commit v4 on v3

--- a/solution.py
+++ b/solution.py
@@ -37,27 +37,25 @@
     return z // z_low, z % z_low, dp % CORES, pos // pos_low, pos % pos_low
 
 
-def select_kernel(dims, pos_dev, features_hbm, counts_hbm, order_hbm, *refs):
+def select_kernel(dims, pos_dev, features_hbm, counts_ref, order_hbm, *refs):
     pos_low, pos_high = dims
-    *out_refs, features_ref, counts_ref, order_ref, picked_ref, sems = refs
-    copies = [
-        pltpu.make_async_copy(source, target, sems.at[i])
-        for i, (source, target) in enumerate(
-            ((features_hbm, features_ref), (order_hbm, order_ref), (counts_hbm, counts_ref))
-        )
-    ]
-    for copy in copies:
+    *out_refs, features_ref, order_ref, picked_ref, sems = refs
+    order_copy = pltpu.make_async_copy(order_hbm, order_ref, sems.at[0])
+    feature_copies = [pltpu.make_async_copy(features_hbm, features_ref, sems.at[1])]
+    for copy in feature_copies:
         copy.start()
+    order_copy.start()
     slots, channels, positions = features_ref.shape
     x = lax.axis_index("pos") % pos_low
     lane = lax.broadcasted_iota(jnp.int32, (channels, LANES), 1)
     row = lax.broadcasted_iota(jnp.int32, (channels, LANES), 0)
     flag = lax.broadcasted_iota(jnp.int32, (positions, LANES), 1) == CH
-    for copy in reversed(copies):
-        copy.wait()
+    owned = counts_ref[0]
+    order_copy.wait()
     order = order_ref[...].reshape(1, channels)[:, :LANES]
     picker = jnp.where((row == order) & (lane < CH), 1.0, 0.0).astype(jnp.bfloat16)
-    owned = counts_ref[0]
+    for copy in feature_copies:
+        copy.wait()
     for slot in range(slots):
         picked = lax.dot_general(
             features_ref[slot], picker, (((0,), (0,)), ((), ())), preferred_element_type=jnp.float32
@@ -140,13 +138,14 @@
             centered = samples - mean * live
             high = centered.astype(jnp.bfloat16)
             low = (centered - high.astype(jnp.float32)).astype(jnp.bfloat16)
+            both = jnp.swapaxes(jnp.concatenate([high, low], axis=0), 0, 1)[:tall]
             sums = lax.dot_general(
-                jnp.concatenate([high, high, low], axis=0),
-                jnp.concatenate([high, low, high], axis=0),
-                (((0,), (0,)), ((), ())),
+                jnp.concatenate([both, both], axis=1),
+                jnp.concatenate([high, high, low, jnp.zeros_like(low)], axis=0),
+                (((1,), (0,)), ((), ())),
                 preferred_element_type=jnp.float32,
             )
-            turn_ref[group, pl.ds(row, tall, stride=PITCH), :] = sums[:tall] * factor + ridge
+            turn_ref[group, pl.ds(row, tall, stride=PITCH), :] = sums * factor + ridge
         for channel in range(CH):
             cov_ref[group, channel] = turn_ref[group, pl.ds(channel * PITCH, ROWS), :CH]
         out(group).start()
@@ -191,14 +190,13 @@
     parts = pl.pallas_call(
         functools.partial(select_kernel, (pos_low, pos_high), pos_dev),
         out_shape=[jax.ShapeDtypeStruct((half, LANES), wire)] * pos_low,
-        in_specs=[hbm] * 3,
+        in_specs=[hbm, pl.BlockSpec(memory_space=pltpu.SMEM), hbm],
         out_specs=[vmem] * pos_low,
         scratch_shapes=[
             pltpu.VMEM((slots, channels, positions), wire),
-            pltpu.SMEM((1,), jnp.int32),
             pltpu.VMEM((channels,), jnp.int32),
             pltpu.VMEM((slots, positions, LANES), jnp.float32),
-            pltpu.SemaphoreType.DMA((3,)),
+            pltpu.SemaphoreType.DMA((1 + slots,)),
         ],
         compiler_params=pltpu.CompilerParams(vmem_limit_bytes=16 * MIB),
     )(

time: 21.8 us -> 21.7 us (level)
  no operation moved by 1% of the time
where the time goes in v4:
time: 21.7 us; the launch traced here: 21.5 us
  starting transfers between devices  10.2 us (47%)
  waiting for transfers between devices  7 us (32%)
  Pallas kernels  3 us (14%)
  between operations  1.3 us (6%)
    ppermute x10, starting transfers between devices, send(): return lax.ppermute(block, ('dp', 'pos'), pairs)  10.2 us
    ppermute x10, waiting for transfers between devices, send(): return lax.ppermute(block, ('dp', 'pos'), pairs)  7 us
    pallas_call x1, Pallas kernels, on_device(): pl.pallas_call(functools.partial(stats_kernel, dims, images, pos_dev), ou...  1.77 us
    pallas_call x1, Pallas kernels, on_device(): pl.pallas_call(functools.partial(select_kernel, (pos_low, pos_high), pos_...  1.17 us
  transfers between devices with their start and end apart: 10, of which 5 were waited for; matrix products, arithmetic and copies ran while one was open for 0% of the time, Pallas kernels for 0%

profile of v4, /device:TPU:0, one launch (start us, length us, event | category | flops | bytes accessed | tf_op | source)
XLA Modules:
  0.0 21.5 jit_solution(13121080880650770519)
XLA Ops:
  1.3 1.2 %shard_map.50 = (bf16[128,128]{1,0:T(8,128)(2,1)S(1)}, bf16[128,128]{1,0:T(8,128)(2,1)S(1)}) custom-call(bf16[2,224,128]{2,1,0:T(8,128)(2,1)} %bitcast.2, s32[1]{0:T(128)S(6)} %copy.5.counts_ref, s32[224]{0:T(256)} %order_hbm.1), custom_call_target="tpu_custom_call" | custom-call | tf_op jit(solution)/shard_map/pallas_call | solution.py:190
  2.4 3.5 %collective-permute-start = (bf16[128,128]{1,0:T(8,128)(2,1)S(1)}, bf16[128,128]{1,0:T(8,128)(2,1)S(1)}, u32[]{:S(2)}, u32[]{:S(2)}) collective-permute-start(bf16[128,128]{1,0:T(8,128)(2,1)S(1)} %get-tuple-element.8.refs_0_), channel_id=1, source_target_pairs={{0,20},{1,21},{2,22},{3,23},{4,16},{5,17},{6,18},{7,19},{8,28},{9,... | collective-permute-start | bytes 98312 | tf_op jit(solution)/shard_map/ppermute | solution.py:187
  6.0 1.5 %collective-permute-start.2 = (bf16[128,128]{1,0:T(8,128)(2,1)S(1)}, bf16[128,128]{1,0:T(8,128)(2,1)S(1)}, u32[]{:S(2)}, u32[]{:S(2)}) collective-permute-start(bf16[128,128]{1,0:T(8,128)(2,1)S(1)} %get-tuple-element.9), channel_id=1, source_target_pairs={{0,21},{1,20},{2,23},{3,22},{4,17},{5,16},{6,19},{7,18},{8,29},{9,... | collective-permute-start | bytes 98312 | tf_op jit(solution)/shard_map/ppermute | solution.py:187
  7.5 0.3 %collective-permute-start.1 = (bf16[128,128]{1,0:T(8,128)(2,1)S(1)}, bf16[128,128]{1,0:T(8,128)(2,1)S(1)}, u32[]{:S(2)}, u32[]{:S(2)}) collective-permute-start(bf16[128,128]{1,0:T(8,128)(2,1)S(1)} %get-tuple-element.9), channel_id=1, source_target_pairs={{0,5},{1,4},{2,7},{3,6},{4,1},{5,0},{6,3},{7,2},{8,13},{9,12},{10,... | collective-permute-start | bytes 98312 | tf_op jit(solution)/shard_map/ppermute | solution.py:187
  7.8 0.0 collective-permute-done.refs_1_
  7.8 3.4 %collective-permute-done.2.refs_3_ = bf16[128,128]{1,0:T(8,128)(2,1)S(1)} collective-permute-done((bf16[128,128]{1,0:T(8,128)(2,1)S(1)}, bf16[128,128]{1,0:T(8,128)(2,1)S(1)}, u32[]{:S(2)}, u32[]{:S(2)}) %collective-permute-start.2) | collective-permute-done | bytes 32800 | tf_op jit(solution)/shard_map/ppermute | solution.py:187
  11.2 0.0 collective-permute-done.1.refs_2_
  11.3 0.1 shard_map.51
  11.3 2.8 %collective-permute-start.8 = (bf16[256,128]{1,0:T(8,128)(2,1)S(1)}, bf16[256,128]{1,0:T(8,128)(2,1)S(1)}, u32[]{:S(2)}, u32[]{:S(2)}) collective-permute-start(bf16[256,128]{1,0:T(8,128)(2,1)S(1)} %get-tuple-element.11), channel_id=1, source_target_pairs={{0,14},{1,15},{2,12},{3,13},{4,10},{5,11},{6,8},{7,9},{8,6},{9,7},... | collective-permute-start | bytes 196616 | tf_op jit(solution)/shard_map/ppermute | solution.py:187
  14.1 0.1 collective-permute-start.6
  14.2 0.9 %collective-permute-start.4 = (bf16[256,128]{1,0:T(8,128)(2,1)S(1)}, bf16[256,128]{1,0:T(8,128)(2,1)S(1)}, u32[]{:S(2)}, u32[]{:S(2)}) collective-permute-start(bf16[256,128]{1,0:T(8,128)(2,1)S(1)} %get-tuple-element.10.refs_0_), channel_id=1, source_target_pairs={{0,12},{1,13},{2,14},{3,15},{4,8},{5,9},{6,10},{7,11},{8,4},{9,5},... | collective-permute-start | bytes 196616 | tf_op jit(solution)/shard_map/ppermute | solution.py:187
  15.1 0.0 collective-permute-start.3
  15.1 1.2 %collective-permute-done.8.refs_6_ = bf16[256,128]{1,0:T(8,128)(2,1)S(1)} collective-permute-done((bf16[256,128]{1,0:T(8,128)(2,1)S(1)}, bf16[256,128]{1,0:T(8,128)(2,1)S(1)}, u32[]{:S(2)}, u32[]{:S(2)}) %collective-permute-start.8) | collective-permute-done | bytes 65568 | tf_op jit(solution)/shard_map/ppermute | solution.py:187
  16.3 0.5 %collective-permute-start.9 = (bf16[256,128]{1,0:T(8,128)(2,1)S(1)}, bf16[256,128]{1,0:T(8,128)(2,1)S(1)}, u32[]{:S(2)}, u32[]{:S(2)}) collective-permute-start(bf16[256,128]{1,0:T(8,128)(2,1)S(1)} %collective-permute-done.8.refs_6_), channel_id=1, source_target_pairs={{0,4},{1,5},{2,6},{3,7},{4,0},{5,1},{6,2},{7,3},{8,12},{9,13},{10,... | collective-permute-start | bytes 196616 | tf_op jit(solution)/shard_map/ppermute | solution.py:187
  16.9 1.4 %collective-permute-done.6.refs_4_ = bf16[256,128]{1,0:T(8,128)(2,1)S(1)} collective-permute-done((bf16[256,128]{1,0:T(8,128)(2,1)S(1)}, bf16[256,128]{1,0:T(8,128)(2,1)S(1)}, u32[]{:S(2)}, u32[]{:S(2)}) %collective-permute-start.6) | collective-permute-done | bytes 65568 | tf_op jit(solution)/shard_map/ppermute | solution.py:187
  18.3 0.1 collective-permute-start.7
  18.4 0.0 collective-permute-done.4.refs_2_
  18.4 0.4 %collective-permute-start.5 = (bf16[256,128]{1,0:T(8,128)(2,1)S(1)}, bf16[256,128]{1,0:T(8,128)(2,1)S(1)}, u32[]{:S(2)}, u32[]{:S(2)}) collective-permute-start(bf16[256,128]{1,0:T(8,128)(2,1)S(1)} %collective-permute-done.4.refs_2_), channel_id=1, source_target_pairs={{0,4},{1,5},{2,6},{3,7},{4,0},{5,1},{6,2},{7,3},{8,12},{9,13},{10,... | collective-permute-start | bytes 196616 | tf_op jit(solution)/shard_map/ppermute | solution.py:187
  18.8 0.0 collective-permute-done.3.refs_1_
  18.8 0.0 collective-permute-done.9.refs_7_
  18.8 0.7 %collective-permute-done.7.refs_5_ = bf16[256,128]{1,0:T(8,128)(2,1)S(1)} collective-permute-done((bf16[256,128]{1,0:T(8,128)(2,1)S(1)}, bf16[256,128]{1,0:T(8,128)(2,1)S(1)}, u32[]{:S(2)}, u32[]{:S(2)}) %collective-permute-start.7) | collective-permute-done | bytes 65568 | tf_op jit(solution)/shard_map/ppermute | solution.py:187
  19.6 0.2 collective-permute-done.5.refs_3_
  19.7 1.8 %shard_map.52 = (f32[32,100]{1,0:T(8,128)}, f32[100,32,100]{2,1,0:T(8,128)}) custom-call(bf16[256,128]{1,0:T(8,128)(2,1)S(1)} %get-tuple-element.10.refs_0_, bf16[256,128]{1,0:T(8,128)(2,1)S(1)} %collective-permute-done.3.refs_1_, bf16[256,128]{1,0:T(8,128)(2,1)S(1)} %collective-permute-done.4.refs_2_, bf16[256,128]{1,0:T(8,128)(2,1)S(1)} %collective-permute-done.5.refs_3_, ...), custom_call_target="tpu_custom_call" | custom-call | tf_op jit(solution)/shard_map/pallas_call | solution.py:230
Async XLA Ops:
  2.4 5.4 %collective-permute-start = (bf16[128,128]{1,0:T(8,128)(2,1)S(1)}, bf16[128,128]{1,0:T(8,128)(2,1)S(1)}, u32[]{:S(2)}, u32[]{:S(2)}) collective-permute-start(bf16[128,128]{1,0:T(8,128)(2,1)S(1)} %get-tuple-element.8.refs_0_), channel_id=1, source_target_pairs={{0,20},{1,21},{2,22},{3,23},{4,16},{5,17},{6,18},{7,19},{8,28},{9,... | collective-permute-start | bytes 98312 | tf_op jit(solution)/shard_map/ppermute | solution.py:187
  6.0 5.2 %collective-permute-start.2 = (bf16[128,128]{1,0:T(8,128)(2,1)S(1)}, bf16[128,128]{1,0:T(8,128)(2,1)S(1)}, u32[]{:S(2)}, u32[]{:S(2)}) collective-permute-start(bf16[128,128]{1,0:T(8,128)(2,1)S(1)} %get-tuple-element.9), channel_id=1, source_target_pairs={{0,21},{1,20},{2,23},{3,22},{4,17},{5,16},{6,19},{7,18},{8,29},{9,... | collective-permute-start | bytes 98312 | tf_op jit(solution)/shard_map/ppermute | solution.py:187
  7.5 3.7 %collective-permute-start.1 = (bf16[128,128]{1,0:T(8,128)(2,1)S(1)}, bf16[128,128]{1,0:T(8,128)(2,1)S(1)}, u32[]{:S(2)}, u32[]{:S(2)}) collective-permute-start(bf16[128,128]{1,0:T(8,128)(2,1)S(1)} %get-tuple-element.9), channel_id=1, source_target_pairs={{0,5},{1,4},{2,7},{3,6},{4,1},{5,0},{6,3},{7,2},{8,13},{9,12},{10,... | collective-permute-start | bytes 98312 | tf_op jit(solution)/shard_map/ppermute | solution.py:187
  11.3 5.0 %collective-permute-start.8 = (bf16[256,128]{1,0:T(8,128)(2,1)S(1)}, bf16[256,128]{1,0:T(8,128)(2,1)S(1)}, u32[]{:S(2)}, u32[]{:S(2)}) collective-permute-start(bf16[256,128]{1,0:T(8,128)(2,1)S(1)} %get-tuple-element.11), channel_id=1, source_target_pairs={{0,14},{1,15},{2,12},{3,13},{4,10},{5,11},{6,8},{7,9},{8,6},{9,7},... | collective-permute-start | bytes 196616 | tf_op jit(solution)/shard_map/ppermute | solution.py:187
  14.1 4.2 %collective-permute-start.6 = (bf16[256,128]{1,0:T(8,128)(2,1)S(1)}, bf16[256,128]{1,0:T(8,128)(2,1)S(1)}, u32[]{:S(2)}, u32[]{:S(2)}) collective-permute-start(bf16[256,128]{1,0:T(8,128)(2,1)S(1)} %get-tuple-element.11), channel_id=1, source_target_pairs={{0,6},{1,7},{2,4},{3,5},{4,2},{5,3},{6,0},{7,1},{8,14},{9,15},{10,... | collective-permute-start | bytes 196616 | tf_op jit(solution)/shard_map/ppermute | solution.py:187
  14.2 4.3 %collective-permute-start.4 = (bf16[256,128]{1,0:T(8,128)(2,1)S(1)}, bf16[256,128]{1,0:T(8,128)(2,1)S(1)}, u32[]{:S(2)}, u32[]{:S(2)}) collective-permute-start(bf16[256,128]{1,0:T(8,128)(2,1)S(1)} %get-tuple-element.10.refs_0_), channel_id=1, source_target_pairs={{0,12},{1,13},{2,14},{3,15},{4,8},{5,9},{6,10},{7,11},{8,4},{9,5},... | collective-permute-start | bytes 196616 | tf_op jit(solution)/shard_map/ppermute | solution.py:187
  15.1 3.7 %collective-permute-start.3 = (bf16[256,128]{1,0:T(8,128)(2,1)S(1)}, bf16[256,128]{1,0:T(8,128)(2,1)S(1)}, u32[]{:S(2)}, u32[]{:S(2)}) collective-permute-start(bf16[256,128]{1,0:T(8,128)(2,1)S(1)} %get-tuple-element.10.refs_0_), channel_id=1, source_target_pairs={{0,4},{1,5},{2,6},{3,7},{4,0},{5,1},{6,2},{7,3},{8,12},{9,13},{10,... | collective-permute-start | bytes 196616 | tf_op jit(solution)/shard_map/ppermute | solution.py:187
  16.3 2.5 %collective-permute-start.9 = (bf16[256,128]{1,0:T(8,128)(2,1)S(1)}, bf16[256,128]{1,0:T(8,128)(2,1)S(1)}, u32[]{:S(2)}, u32[]{:S(2)}) collective-permute-start(bf16[256,128]{1,0:T(8,128)(2,1)S(1)} %collective-permute-done.8.refs_6_), channel_id=1, source_target_pairs={{0,4},{1,5},{2,6},{3,7},{4,0},{5,1},{6,2},{7,3},{8,12},{9,13},{10,... | collective-permute-start | bytes 196616 | tf_op jit(solution)/shard_map/ppermute | solution.py:187
  18.3 1.3 %collective-permute-start.7 = (bf16[256,128]{1,0:T(8,128)(2,1)S(1)}, bf16[256,128]{1,0:T(8,128)(2,1)S(1)}, u32[]{:S(2)}, u32[]{:S(2)}) collective-permute-start(bf16[256,128]{1,0:T(8,128)(2,1)S(1)} %collective-permute-done.6.refs_4_), channel_id=1, source_target_pairs={{0,4},{1,5},{2,6},{3,7},{4,0},{5,1},{6,2},{7,3},{8,12},{9,13},{10,... | collective-permute-start | bytes 196616 | tf_op jit(solution)/shard_map/ppermute | solution.py:187
  18.4 1.3 %collective-permute-start.5 = (bf16[256,128]{1,0:T(8,128)(2,1)S(1)}, bf16[256,128]{1,0:T(8,128)(2,1)S(1)}, u32[]{:S(2)}, u32[]{:S(2)}) collective-permute-start(bf16[256,128]{1,0:T(8,128)(2,1)S(1)} %collective-permute-done.4.refs_2_), channel_id=1, source_target_pairs={{0,4},{1,5},{2,6},{3,7},{4,0},{5,1},{6,2},{7,3},{8,12},{9,13},{10,... | collective-permute-start | bytes 196616 | tf_op jit(solution)/shard_map/ppermute | solution.py:187

commit v5 on v4

--- a/solution.py
+++ b/solution.py
@@ -13,6 +13,24 @@
 ROWS = 8
 PITCH = ROWS + 1
 MIB = 1 << 20
+PIECES = 4
+PIECE = CH // PIECES
+
+
+def packing(pos_dev):
+    extra = (pos_dev - 1) // (PIECES + 1)
+    return pos_dev - extra, extra
+
+
+def unpack(ref, images, pos_dev):
+    block = ref[...].astype(jnp.float32)
+    size = packing(pos_dev)[1] * images
+    place = lax.broadcasted_iota(jnp.int32, (size, LANES), 1) // PIECE
+    moved = None
+    for piece in range(PIECES):
+        part = pltpu.roll(block[piece * size : (piece + 1) * size], LANES - CH + piece * PIECE, 1)
+        moved = part if moved is None else jnp.where(place == piece, part, moved)
+    return jnp.concatenate([block, moved], axis=0).reshape(pos_dev, images, LANES)
 
 
 def shift(index, n, step, sign=1):
@@ -88,30 +106,59 @@
                 scratch[step, pl.ds(owner * slots + slot, pos_dev, stride=images), :] = block[
                     slot * pos_dev : (slot + 1) * pos_dev
                 ]
-        out_ref[...] = scratch[step].astype(jnp.bfloat16)
-
-
-def stats_kernel(dims, images, pos_dev, *refs):
+        base, extra = packing(pos_dev)
+        size_extra = extra * images
+        own = lax.broadcasted_iota(jnp.int32, (size_extra, LANES), 1) < CH
+        moved = scratch[step, pl.ds(base * images, size_extra), :]
+        for piece in range(PIECES):
+            rows = pl.ds(piece * size_extra, size_extra)
+            turned = pltpu.roll(moved, CH - piece * PIECE, 1)
+            out_ref[rows, :] = jnp.where(own, scratch[step, rows, :], turned).astype(jnp.bfloat16)
+        rows = pl.ds(PIECES * size_extra, base * images - PIECES * size_extra)
+        out_ref[rows, :] = scratch[step, rows, :].astype(jnp.bfloat16)
+
+
+def places(dims, images):
     z_low, z_high, pos_low, pos_high = dims
-    blocks = pos_high * z_low * CORES
-    in_refs = refs[:blocks]
-    mean_hbm, cov_hbm, held, mean_ref, cov_ref, turn_ref, sems = refs[blocks:]
     z_top, z, core, _, _ = coordinates(lax.axis_index("dp"), lax.axis_index("pos"), (z_low, pos_low))
     slot = lax.broadcasted_iota(jnp.int32, (1, images, LANES), 1)
     kept = slot // (images // (z_high * pos_low)) == z_top * pos_low
-    for pair in range(blocks // CORES):
-        pos_step, z_step = pair // z_low, pair % z_low
-        base = (shift(z, z_low, z_step, -1) * pos_high + pos_step) * CORES
-        near = core if pair == 0 else 1 - core
-        first, second = (
-            in_refs[pair * CORES + i][...].astype(jnp.float32).reshape(pos_dev, images, LANES)
-            for i in range(CORES)
-        )
-        held[base + near] = jnp.where(kept, first, second)
-        held[base + 1 - near] = jnp.where(kept, second, first)
+    where = {}
+    for p in range(pos_high):
+        for step in range(z_low):
+            index = (shift(z, z_low, step, -1) * pos_high + p) * CORES
+            near = core if p + step == 0 else 1 - core
+            where[p, step] = (index + near, index + 1 - near)
+    return kept, where
+
+
+def put(held, kept, where, first, second):
+    held[where[0]] = jnp.where(kept, first, second)
+    held[where[1]] = jnp.where(kept, second, first)
+
+
+def prepare_kernel(dims, images, pos_dev, whole, half, *refs):
+    *in_refs, held = refs
+    kept, where = places(dims, images)
+    for i, step in enumerate(whole):
+        first, second = (unpack(in_refs[CORES * i + j], images, pos_dev) for j in range(CORES))
+        put(held, kept, where[step], first, second)
+    for i, step in enumerate(half):
+        held[where[step][0]] = unpack(in_refs[CORES * len(whole) + i], images, pos_dev)
+
+
+def stats_kernel(dims, images, pos_dev, half, *refs):
+    z_low, z_high, pos_low, pos_high = dims
+    blocks = pos_high * z_low * CORES
+    _, *in_refs = refs[: 1 + len(half)]
+    mean_hbm, cov_hbm, held, mean_ref, cov_ref, turn_ref, sems = refs[1 + len(half) :]
+    kept, where = places(dims, images)
+    for step, ref in zip(half, in_refs):
+        put(held, kept, where[step], held[where[step][0]], unpack(ref, images, pos_dev))
+    base = packing(pos_dev)[0]
     everyone = blocks * images
     live = jnp.broadcast_to(
-        held[:, 0].reshape(everyone, LANES)[:, CH : CH + 1], (everyone, LANES)
+        held[:, base - 1].reshape(everyone, LANES)[:, CH : CH + 1], (everyone, LANES)
     )
     total = jnp.sum(live, axis=0, keepdims=True)
     factor = 1.0 / (total - 1.0)
@@ -211,7 +258,7 @@
 
     owns = pl.pallas_call(
         functools.partial(merge_kernel, dims, slots, pos_dev),
-        out_shape=[jax.ShapeDtypeStruct((pos_dev * images, LANES), wire)] * pos_high,
+        out_shape=[jax.ShapeDtypeStruct((packing(pos_dev)[0] * images, LANES), wire)] * pos_high,
         in_specs=[vmem] * (pos_low * z_high),
         out_specs=[vmem] * pos_high,
         scratch_shapes=[pltpu.VMEM((pos_high, pos_dev * images, LANES), jnp.float32)],
@@ -221,29 +268,43 @@
     near = {(0, 0): owns[0]}
     for step in far_first(pos_high, z_low):
         near[step] = send(owns[step[0]], pos_high_step=step[0], z_low_step=step[1], core_step=1)
-    arrays = []
-    for p in range(pos_high):
-        for z in range(z_low):
-            arrays += [near[p, z], send(near[p, z], core_step=1)]
+    other = {step: send(near[step], core_step=1) for step in near}
+    steps = [(0, 0), *far_first(pos_high, z_low)]
+    count = max(1, len(steps) // 2)
+    whole, half = steps[:count], steps[count:]
+    held = jax.ShapeDtypeStruct((pos_high * z_low * CORES, pos_dev, images, LANES), jnp.float32)
+    early = [block for step in whole for block in (near[step], other[step])]
+    early += [near[step] for step in half]
+    ready = pl.pallas_call(
+        functools.partial(prepare_kernel, dims, images, pos_dev, whole, half),
+        out_shape=held,
+        in_specs=[vmem] * len(early),
+        out_specs=vmem,
+        cost_estimate=pl.CostEstimate(
+            flops=0, bytes_accessed=6 * held.size, transcendentals=0
+        ),
+        compiler_params=pltpu.CompilerParams(vmem_limit_bytes=8 * MIB),
+    )(*early)
 
     tall = -(-CH // ROWS) * ROWS
-    mean, covariance = pl.pallas_call(
-        functools.partial(stats_kernel, dims, images, pos_dev),
+    mean, covariance, _ = pl.pallas_call(
+        functools.partial(stats_kernel, dims, images, pos_dev, half),
         out_shape=[
             jax.ShapeDtypeStruct((pos_dev, CH), jnp.float32),
             jax.ShapeDtypeStruct((CH, pos_dev, CH), jnp.float32),
+            held,
         ],
-        in_specs=[vmem] * len(arrays),
-        out_specs=[hbm, hbm],
+        in_specs=[vmem] * (1 + len(half)),
+        out_specs=[hbm, hbm, vmem],
+        input_output_aliases={0: 2},
         scratch_shapes=[
-            pltpu.VMEM((len(arrays), pos_dev, images, LANES), jnp.float32),
             pltpu.VMEM((pos_dev, CH), jnp.float32),
             pltpu.VMEM((pos_dev // ROWS, CH, ROWS, CH), jnp.float32),
             pltpu.VMEM((pos_dev // ROWS, tall * PITCH, LANES), jnp.float32),
             pltpu.SemaphoreType.DMA((pos_dev // ROWS + 1,)),
         ],
-        compiler_params=pltpu.CompilerParams(vmem_limit_bytes=48 * MIB),
-    )(*arrays)
+        compiler_params=pltpu.CompilerParams(vmem_limit_bytes=32 * MIB),
+    )(ready, *(other[step] for step in half))
     return mean, jnp.transpose(covariance, (1, 0, 2))
 
 

time: 21.7 us -> 21.5 us (level)
  waiting for transfers between devices: 7 us -> 6.42 us
  Pallas kernels: 3 us -> 3.25 us
    ppermute x10, waiting for transfers between devices: 7 us -> 6.42 us  [send(): return lax.ppermute(block, ('dp', 'pos'), pairs)]
    pallas_call x1 -> x2, Pallas kernels: 1.77 us -> 1.94 us  [the longest x1 1.78 us: on_device(): pl.pallas_call(functools.partial(stats_kernel, dims, images, pos_dev, hal...]
  transfers between devices with their start and end apart: 10 -> 10, of which waited for: 5 -> 5; matrix products, arithmetic and copies ran while one was open for 0% -> 0% of each run, Pallas kernels for 0% -> 1%
where the time goes in v5:
time: 21.5 us; the launch traced here: 21.3 us
  starting transfers between devices  10.3 us (48%)
  waiting for transfers between devices  6.42 us (30%)
  Pallas kernels  3.25 us (15%)
  between operations  1.31 us (6%)
    ppermute x10, starting transfers between devices, send(): return lax.ppermute(block, ('dp', 'pos'), pairs)  10.3 us
    ppermute x10, waiting for transfers between devices, send(): return lax.ppermute(block, ('dp', 'pos'), pairs)  6.42 us
    pallas_call x1, Pallas kernels, on_device(): pl.pallas_call(functools.partial(stats_kernel, dims, images, pos_dev, hal...  1.78 us
    pallas_call x1, Pallas kernels, on_device(): pl.pallas_call(functools.partial(select_kernel, (pos_low, pos_high), pos_...  1.17 us
  transfers between devices with their start and end apart: 10, of which 5 were waited for; matrix products, arithmetic and copies ran while one was open for 0% of the time, Pallas kernels for 1%

profile of v5, /device:TPU:0, one launch (start us, length us, event | category | flops | bytes accessed | tf_op | source)
XLA Modules:
  0.0 21.3 jit_solution(9286519796176639912)
XLA Ops:
  1.3 1.2 %shard_map.50 = (bf16[128,128]{1,0:T(8,128)(2,1)S(1)}, bf16[128,128]{1,0:T(8,128)(2,1)S(1)}) custom-call(bf16[2,224,128]{2,1,0:T(8,128)(2,1)} %bitcast.2, s32[1]{0:T(128)S(6)} %copy.7.counts_ref, s32[224]{0:T(256)} %order_hbm.1), custom_call_target="tpu_custom_call" | custom-call | tf_op jit(solution)/shard_map/pallas_call | solution.py:237
  2.4 3.5 %collective-permute-start = (bf16[128,128]{1,0:T(8,128)(2,1)S(1)}, bf16[128,128]{1,0:T(8,128)(2,1)S(1)}, u32[]{:S(2)}, u32[]{:S(2)}) collective-permute-start(bf16[128,128]{1,0:T(8,128)(2,1)S(1)} %get-tuple-element.8.refs_0_), channel_id=1, source_target_pairs={{0,20},{1,21},{2,22},{3,23},{4,16},{5,17},{6,18},{7,19},{8,28},{9,... | collective-permute-start | bytes 98312 | tf_op jit(solution)/shard_map/ppermute | solution.py:234
  6.0 1.5 %collective-permute-start.2 = (bf16[128,128]{1,0:T(8,128)(2,1)S(1)}, bf16[128,128]{1,0:T(8,128)(2,1)S(1)}, u32[]{:S(2)}, u32[]{:S(2)}) collective-permute-start(bf16[128,128]{1,0:T(8,128)(2,1)S(1)} %get-tuple-element.9), channel_id=1, source_target_pairs={{0,21},{1,20},{2,23},{3,22},{4,17},{5,16},{6,19},{7,18},{8,29},{9,... | collective-permute-start | bytes 98312 | tf_op jit(solution)/shard_map/ppermute | solution.py:234
  7.5 0.3 %collective-permute-start.1 = (bf16[128,128]{1,0:T(8,128)(2,1)S(1)}, bf16[128,128]{1,0:T(8,128)(2,1)S(1)}, u32[]{:S(2)}, u32[]{:S(2)}) collective-permute-start(bf16[128,128]{1,0:T(8,128)(2,1)S(1)} %get-tuple-element.9), channel_id=1, source_target_pairs={{0,5},{1,4},{2,7},{3,6},{4,1},{5,0},{6,3},{7,2},{8,13},{9,12},{10,... | collective-permute-start | bytes 98312 | tf_op jit(solution)/shard_map/ppermute | solution.py:234
  7.8 0.0 collective-permute-done.refs_1_
  7.8 3.4 %collective-permute-done.2.refs_3_ = bf16[128,128]{1,0:T(8,128)(2,1)S(1)} collective-permute-done((bf16[128,128]{1,0:T(8,128)(2,1)S(1)}, bf16[128,128]{1,0:T(8,128)(2,1)S(1)}, u32[]{:S(2)}, u32[]{:S(2)}) %collective-permute-start.2) | collective-permute-done | bytes 32800 | tf_op jit(solution)/shard_map/ppermute | solution.py:234
  11.2 0.0 collective-permute-done.1.refs_2_
  11.3 0.1 shard_map.51
  11.4 2.8 %collective-permute-start.4 = (bf16[208,128]{1,0:T(8,128)(2,1)S(1)}, bf16[208,128]{1,0:T(8,128)(2,1)S(1)}, u32[]{:S(2)}, u32[]{:S(2)}) collective-permute-start(bf16[208,128]{1,0:T(8,128)(2,1)S(1)} %get-tuple-element.11), channel_id=1, source_target_pairs={{0,14},{1,15},{2,12},{3,13},{4,10},{5,11},{6,8},{7,9},{8,6},{9,7},... | collective-permute-start | bytes 159752 | tf_op jit(solution)/shard_map/ppermute | solution.py:234
  14.2 0.1 collective-permute-start.7
  14.2 0.9 %collective-permute-start.6 = (bf16[208,128]{1,0:T(8,128)(2,1)S(1)}, bf16[208,128]{1,0:T(8,128)(2,1)S(1)}, u32[]{:S(2)}, u32[]{:S(2)}) collective-permute-start(bf16[208,128]{1,0:T(8,128)(2,1)S(1)} %get-tuple-element.10.refs_0_), channel_id=1, source_target_pairs={{0,12},{1,13},{2,14},{3,15},{4,8},{5,9},{6,10},{7,11},{8,4},{9,5},... | collective-permute-start | bytes 159752 | tf_op jit(solution)/shard_map/ppermute | solution.py:234
  15.2 0.0 collective-permute-start.3
  15.2 1.0 %collective-permute-done.4.refs_2_ = bf16[208,128]{1,0:T(8,128)(2,1)S(1)} collective-permute-done((bf16[208,128]{1,0:T(8,128)(2,1)S(1)}, bf16[208,128]{1,0:T(8,128)(2,1)S(1)}, u32[]{:S(2)}, u32[]{:S(2)}) %collective-permute-start.4) | collective-permute-done | bytes 53280 | tf_op jit(solution)/shard_map/ppermute | solution.py:234
  16.2 0.7 %collective-permute-start.5 = (bf16[208,128]{1,0:T(8,128)(2,1)S(1)}, bf16[208,128]{1,0:T(8,128)(2,1)S(1)}, u32[]{:S(2)}, u32[]{:S(2)}) collective-permute-start(bf16[208,128]{1,0:T(8,128)(2,1)S(1)} %collective-permute-done.4.refs_2_), channel_id=1, source_target_pairs={{0,4},{1,5},{2,6},{3,7},{4,0},{5,1},{6,2},{7,3},{8,12},{9,13},{10,... | collective-permute-start | bytes 159752 | tf_op jit(solution)/shard_map/ppermute | solution.py:234
  16.8 1.3 %collective-permute-done.7.refs_5_ = bf16[208,128]{1,0:T(8,128)(2,1)S(1)} collective-permute-done((bf16[208,128]{1,0:T(8,128)(2,1)S(1)}, bf16[208,128]{1,0:T(8,128)(2,1)S(1)}, u32[]{:S(2)}, u32[]{:S(2)}) %collective-permute-start.7) | collective-permute-done | bytes 53280 | tf_op jit(solution)/shard_map/ppermute | solution.py:234
  18.1 0.1 collective-permute-start.9
  18.3 0.0 collective-permute-done.6.refs_4_
  18.3 0.4 %collective-permute-start.8 = (bf16[208,128]{1,0:T(8,128)(2,1)S(1)}, bf16[208,128]{1,0:T(8,128)(2,1)S(1)}, u32[]{:S(2)}, u32[]{:S(2)}) collective-permute-start(bf16[208,128]{1,0:T(8,128)(2,1)S(1)} %collective-permute-done.6.refs_4_), channel_id=1, source_target_pairs={{0,4},{1,5},{2,6},{3,7},{4,0},{5,1},{6,2},{7,3},{8,12},{9,13},{10,... | collective-permute-start | bytes 159752 | tf_op jit(solution)/shard_map/ppermute | solution.py:234
  18.7 0.0 collective-permute-done.3.refs_1_
  18.7 0.0 collective-permute-done.5.refs_3_
  18.7 0.2 shard_map.52.refs_0_
  18.8 0.5 %collective-permute-done.9.refs_2_ = bf16[208,128]{1,0:T(8,128)(2,1)S(1)} collective-permute-done((bf16[208,128]{1,0:T(8,128)(2,1)S(1)}, bf16[208,128]{1,0:T(8,128)(2,1)S(1)}, u32[]{:S(2)}, u32[]{:S(2)}) %collective-permute-start.9) | collective-permute-done | bytes 53280 | tf_op jit(solution)/shard_map/ppermute | solution.py:234
  19.4 0.2 collective-permute-done.8.refs_1_
  19.5 1.8 %shard_map.53 = (f32[32,100]{1,0:T(8,128)}, f32[100,32,100]{2,1,0:T(8,128)}, f32[8,32,8,128]{3,2,1,0:T(8,128)S(1)}) custom-call(f32[8,32,8,128]{3,2,1,0:T(8,128)S(1)} %shard_map.52.refs_0_, bf16[208,128]{1,0:T(8,128)(2,1)S(1)} %collective-permute-done.8.refs_1_, bf16[208,128]{1,0:T(8,128)(2,1)S(1)} %collective-permute-done.9.refs_2_), custom_call_target="tpu_custom_call", output_to_operand_aliasing={{2}: (0, {})} | custom-call | tf_op jit(solution)/shard_map/pallas_call | solution.py:290
Async XLA Ops:
  2.4 5.4 %collective-permute-start = (bf16[128,128]{1,0:T(8,128)(2,1)S(1)}, bf16[128,128]{1,0:T(8,128)(2,1)S(1)}, u32[]{:S(2)}, u32[]{:S(2)}) collective-permute-start(bf16[128,128]{1,0:T(8,128)(2,1)S(1)} %get-tuple-element.8.refs_0_), channel_id=1, source_target_pairs={{0,20},{1,21},{2,22},{3,23},{4,16},{5,17},{6,18},{7,19},{8,28},{9,... | collective-permute-start | bytes 98312 | tf_op jit(solution)/shard_map/ppermute | solution.py:234
  6.0 5.2 %collective-permute-start.2 = (bf16[128,128]{1,0:T(8,128)(2,1)S(1)}, bf16[128,128]{1,0:T(8,128)(2,1)S(1)}, u32[]{:S(2)}, u32[]{:S(2)}) collective-permute-start(bf16[128,128]{1,0:T(8,128)(2,1)S(1)} %get-tuple-element.9), channel_id=1, source_target_pairs={{0,21},{1,20},{2,23},{3,22},{4,17},{5,16},{6,19},{7,18},{8,29},{9,... | collective-permute-start | bytes 98312 | tf_op jit(solution)/shard_map/ppermute | solution.py:234
  7.5 3.7 %collective-permute-start.1 = (bf16[128,128]{1,0:T(8,128)(2,1)S(1)}, bf16[128,128]{1,0:T(8,128)(2,1)S(1)}, u32[]{:S(2)}, u32[]{:S(2)}) collective-permute-start(bf16[128,128]{1,0:T(8,128)(2,1)S(1)} %get-tuple-element.9), channel_id=1, source_target_pairs={{0,5},{1,4},{2,7},{3,6},{4,1},{5,0},{6,3},{7,2},{8,13},{9,12},{10,... | collective-permute-start | bytes 98312 | tf_op jit(solution)/shard_map/ppermute | solution.py:234
  11.4 4.7 %collective-permute-start.4 = (bf16[208,128]{1,0:T(8,128)(2,1)S(1)}, bf16[208,128]{1,0:T(8,128)(2,1)S(1)}, u32[]{:S(2)}, u32[]{:S(2)}) collective-permute-start(bf16[208,128]{1,0:T(8,128)(2,1)S(1)} %get-tuple-element.11), channel_id=1, source_target_pairs={{0,14},{1,15},{2,12},{3,13},{4,10},{5,11},{6,8},{7,9},{8,6},{9,7},... | collective-permute-start | bytes 159752 | tf_op jit(solution)/shard_map/ppermute | solution.py:234
  14.2 4.0 %collective-permute-start.7 = (bf16[208,128]{1,0:T(8,128)(2,1)S(1)}, bf16[208,128]{1,0:T(8,128)(2,1)S(1)}, u32[]{:S(2)}, u32[]{:S(2)}) collective-permute-start(bf16[208,128]{1,0:T(8,128)(2,1)S(1)} %get-tuple-element.11), channel_id=1, source_target_pairs={{0,6},{1,7},{2,4},{3,5},{4,2},{5,3},{6,0},{7,1},{8,14},{9,15},{10,... | collective-permute-start | bytes 159752 | tf_op jit(solution)/shard_map/ppermute | solution.py:234
  14.2 4.0 %collective-permute-start.6 = (bf16[208,128]{1,0:T(8,128)(2,1)S(1)}, bf16[208,128]{1,0:T(8,128)(2,1)S(1)}, u32[]{:S(2)}, u32[]{:S(2)}) collective-permute-start(bf16[208,128]{1,0:T(8,128)(2,1)S(1)} %get-tuple-element.10.refs_0_), channel_id=1, source_target_pairs={{0,12},{1,13},{2,14},{3,15},{4,8},{5,9},{6,10},{7,11},{8,4},{9,5},... | collective-permute-start | bytes 159752 | tf_op jit(solution)/shard_map/ppermute | solution.py:234
  15.2 3.5 %collective-permute-start.3 = (bf16[208,128]{1,0:T(8,128)(2,1)S(1)}, bf16[208,128]{1,0:T(8,128)(2,1)S(1)}, u32[]{:S(2)}, u32[]{:S(2)}) collective-permute-start(bf16[208,128]{1,0:T(8,128)(2,1)S(1)} %get-tuple-element.10.refs_0_), channel_id=1, source_target_pairs={{0,4},{1,5},{2,6},{3,7},{4,0},{5,1},{6,2},{7,3},{8,12},{9,13},{10,... | collective-permute-start | bytes 159752 | tf_op jit(solution)/shard_map/ppermute | solution.py:234
  16.2 2.5 %collective-permute-start.5 = (bf16[208,128]{1,0:T(8,128)(2,1)S(1)}, bf16[208,128]{1,0:T(8,128)(2,1)S(1)}, u32[]{:S(2)}, u32[]{:S(2)}) collective-permute-start(bf16[208,128]{1,0:T(8,128)(2,1)S(1)} %collective-permute-done.4.refs_2_), channel_id=1, source_target_pairs={{0,4},{1,5},{2,6},{3,7},{4,0},{5,1},{6,2},{7,3},{8,12},{9,13},{10,... | collective-permute-start | bytes 159752 | tf_op jit(solution)/shard_map/ppermute | solution.py:234
  18.1 1.2 %collective-permute-start.9 = (bf16[208,128]{1,0:T(8,128)(2,1)S(1)}, bf16[208,128]{1,0:T(8,128)(2,1)S(1)}, u32[]{:S(2)}, u32[]{:S(2)}) collective-permute-start(bf16[208,128]{1,0:T(8,128)(2,1)S(1)} %collective-permute-done.7.refs_5_), channel_id=1, source_target_pairs={{0,4},{1,5},{2,6},{3,7},{4,0},{5,1},{6,2},{7,3},{8,12},{9,13},{10,... | collective-permute-start | bytes 159752 | tf_op jit(solution)/shard_map/ppermute | solution.py:234
  18.3 1.3 %collective-permute-start.8 = (bf16[208,128]{1,0:T(8,128)(2,1)S(1)}, bf16[208,128]{1,0:T(8,128)(2,1)S(1)}, u32[]{:S(2)}, u32[]{:S(2)}) collective-permute-start(bf16[208,128]{1,0:T(8,128)(2,1)S(1)} %collective-permute-done.6.refs_4_), channel_id=1, source_target_pairs={{0,4},{1,5},{2,6},{3,7},{4,0},{5,1},{6,2},{7,3},{8,12},{9,13},{10,... | collective-permute-start | bytes 159752 | tf_op jit(solution)/shard_map/ppermute | solution.py:234

commit v6 on v5

--- a/solution.py
+++ b/solution.py
@@ -161,7 +161,8 @@
         held[:, base - 1].reshape(everyone, LANES)[:, CH : CH + 1], (everyone, LANES)
     )
     total = jnp.sum(live, axis=0, keepdims=True)
-    factor = 1.0 / (total - 1.0)
+    root = lax.rsqrt(total - 1.0)
+    weight = live * root
     tall = turn_ref.shape[1] // PITCH
     diagonal = lax.broadcasted_iota(jnp.int32, (tall, LANES), 0) == lax.broadcasted_iota(
         jnp.int32, (tall, LANES), 1
@@ -182,7 +183,7 @@
             samples = held[:, position].reshape(everyone, LANES)
             mean = jnp.sum(samples, axis=0, keepdims=True) / total
             mean_ref[pl.ds(position, 1), :] = mean[:, :CH]
-            centered = samples - mean * live
+            centered = samples * root - mean * weight
             high = centered.astype(jnp.bfloat16)
             low = (centered - high.astype(jnp.float32)).astype(jnp.bfloat16)
             both = jnp.swapaxes(jnp.concatenate([high, low], axis=0), 0, 1)[:tall]
@@ -192,17 +193,28 @@
                 (((1,), (0,)), ((), ())),
                 preferred_element_type=jnp.float32,
             )
-            turn_ref[group, pl.ds(row, tall, stride=PITCH), :] = sums * factor + ridge
+            turn_ref[group, pl.ds(row, tall, stride=PITCH), :] = sums + ridge
+        return 0
+
+    def finish(group):
         for channel in range(CH):
             cov_ref[group, channel] = turn_ref[group, pl.ds(channel * PITCH, ROWS), :CH]
         out(group).start()
-        return 0
 
     if everyone > 256:
-        lax.fori_loop(0, groups, one_group, 0)
+
+        def looped(group, carry):
+            one_group(group, carry)
+            finish(group)
+            return carry
+
+        lax.fori_loop(0, groups, looped, 0)
     else:
         for group in range(groups):
             one_group(group, 0)
+            if group:
+                finish(group - 1)
+        finish(groups - 1)
     mean_out = pltpu.make_async_copy(mean_ref, mean_hbm, sems.at[groups])
     mean_out.start()
     for group in range(groups):

time: 21.5 us -> 21.5 us (level)
  no operation moved by 1% of the time
where the time goes in v6:
time: 21.5 us; the launch traced here: 21.3 us
  starting transfers between devices  10.3 us (48%)
  waiting for transfers between devices  6.42 us (30%)
  Pallas kernels  3.25 us (15%)
  between operations  1.31 us (6%)
    ppermute x10, starting transfers between devices, send(): return lax.ppermute(block, ('dp', 'pos'), pairs)  10.3 us
    ppermute x10, waiting for transfers between devices, send(): return lax.ppermute(block, ('dp', 'pos'), pairs)  6.42 us
    pallas_call x1, Pallas kernels, on_device(): pl.pallas_call(functools.partial(stats_kernel, dims, images, pos_dev, hal...  1.78 us
    pallas_call x1, Pallas kernels, on_device(): pl.pallas_call(functools.partial(select_kernel, (pos_low, pos_high), pos_...  1.17 us
  transfers between devices with their start and end apart: 10, of which 5 were waited for; matrix products, arithmetic and copies ran while one was open for 0% of the time, Pallas kernels for 1%

profile of v6, /device:TPU:0, one launch (start us, length us, event | category | flops | bytes accessed | tf_op | source)
XLA Modules:
  0.0 21.3 jit_solution(9716548231282456877)
XLA Ops:
  1.3 1.2 %shard_map.50 = (bf16[128,128]{1,0:T(8,128)(2,1)S(1)}, bf16[128,128]{1,0:T(8,128)(2,1)S(1)}) custom-call(bf16[2,224,128]{2,1,0:T(8,128)(2,1)} %bitcast.2, s32[1]{0:T(128)S(6)} %copy.7.counts_ref, s32[224]{0:T(256)} %order_hbm.1), custom_call_target="tpu_custom_call" | custom-call | tf_op jit(solution)/shard_map/pallas_call | solution.py:249
  2.4 3.5 %collective-permute-start = (bf16[128,128]{1,0:T(8,128)(2,1)S(1)}, bf16[128,128]{1,0:T(8,128)(2,1)S(1)}, u32[]{:S(2)}, u32[]{:S(2)}) collective-permute-start(bf16[128,128]{1,0:T(8,128)(2,1)S(1)} %get-tuple-element.8.refs_0_), channel_id=1, source_target_pairs={{0,20},{1,21},{2,22},{3,23},{4,16},{5,17},{6,18},{7,19},{8,28},{9,... | collective-permute-start | bytes 98312 | tf_op jit(solution)/shard_map/ppermute | solution.py:246
  6.0 1.5 %collective-permute-start.2 = (bf16[128,128]{1,0:T(8,128)(2,1)S(1)}, bf16[128,128]{1,0:T(8,128)(2,1)S(1)}, u32[]{:S(2)}, u32[]{:S(2)}) collective-permute-start(bf16[128,128]{1,0:T(8,128)(2,1)S(1)} %get-tuple-element.9), channel_id=1, source_target_pairs={{0,21},{1,20},{2,23},{3,22},{4,17},{5,16},{6,19},{7,18},{8,29},{9,... | collective-permute-start | bytes 98312 | tf_op jit(solution)/shard_map/ppermute | solution.py:246
  7.5 0.3 %collective-permute-start.1 = (bf16[128,128]{1,0:T(8,128)(2,1)S(1)}, bf16[128,128]{1,0:T(8,128)(2,1)S(1)}, u32[]{:S(2)}, u32[]{:S(2)}) collective-permute-start(bf16[128,128]{1,0:T(8,128)(2,1)S(1)} %get-tuple-element.9), channel_id=1, source_target_pairs={{0,5},{1,4},{2,7},{3,6},{4,1},{5,0},{6,3},{7,2},{8,13},{9,12},{10,... | collective-permute-start | bytes 98312 | tf_op jit(solution)/shard_map/ppermute | solution.py:246
  7.8 0.0 collective-permute-done.refs_1_
  7.8 3.4 %collective-permute-done.2.refs_3_ = bf16[128,128]{1,0:T(8,128)(2,1)S(1)} collective-permute-done((bf16[128,128]{1,0:T(8,128)(2,1)S(1)}, bf16[128,128]{1,0:T(8,128)(2,1)S(1)}, u32[]{:S(2)}, u32[]{:S(2)}) %collective-permute-start.2) | collective-permute-done | bytes 32800 | tf_op jit(solution)/shard_map/ppermute | solution.py:246
  11.2 0.0 collective-permute-done.1.refs_2_
  11.3 0.1 shard_map.51
  11.4 2.8 %collective-permute-start.4 = (bf16[208,128]{1,0:T(8,128)(2,1)S(1)}, bf16[208,128]{1,0:T(8,128)(2,1)S(1)}, u32[]{:S(2)}, u32[]{:S(2)}) collective-permute-start(bf16[208,128]{1,0:T(8,128)(2,1)S(1)} %get-tuple-element.11), channel_id=1, source_target_pairs={{0,14},{1,15},{2,12},{3,13},{4,10},{5,11},{6,8},{7,9},{8,6},{9,7},... | collective-permute-start | bytes 159752 | tf_op jit(solution)/shard_map/ppermute | solution.py:246
  14.2 0.1 collective-permute-start.7
  14.2 0.9 %collective-permute-start.6 = (bf16[208,128]{1,0:T(8,128)(2,1)S(1)}, bf16[208,128]{1,0:T(8,128)(2,1)S(1)}, u32[]{:S(2)}, u32[]{:S(2)}) collective-permute-start(bf16[208,128]{1,0:T(8,128)(2,1)S(1)} %get-tuple-element.10.refs_0_), channel_id=1, source_target_pairs={{0,12},{1,13},{2,14},{3,15},{4,8},{5,9},{6,10},{7,11},{8,4},{9,5},... | collective-permute-start | bytes 159752 | tf_op jit(solution)/shard_map/ppermute | solution.py:246
  15.2 0.0 collective-permute-start.3
  15.2 1.0 %collective-permute-done.4.refs_2_ = bf16[208,128]{1,0:T(8,128)(2,1)S(1)} collective-permute-done((bf16[208,128]{1,0:T(8,128)(2,1)S(1)}, bf16[208,128]{1,0:T(8,128)(2,1)S(1)}, u32[]{:S(2)}, u32[]{:S(2)}) %collective-permute-start.4) | collective-permute-done | bytes 53280 | tf_op jit(solution)/shard_map/ppermute | solution.py:246
  16.2 0.7 %collective-permute-start.5 = (bf16[208,128]{1,0:T(8,128)(2,1)S(1)}, bf16[208,128]{1,0:T(8,128)(2,1)S(1)}, u32[]{:S(2)}, u32[]{:S(2)}) collective-permute-start(bf16[208,128]{1,0:T(8,128)(2,1)S(1)} %collective-permute-done.4.refs_2_), channel_id=1, source_target_pairs={{0,4},{1,5},{2,6},{3,7},{4,0},{5,1},{6,2},{7,3},{8,12},{9,13},{10,... | collective-permute-start | bytes 159752 | tf_op jit(solution)/shard_map/ppermute | solution.py:246
  16.8 1.3 %collective-permute-done.7.refs_5_ = bf16[208,128]{1,0:T(8,128)(2,1)S(1)} collective-permute-done((bf16[208,128]{1,0:T(8,128)(2,1)S(1)}, bf16[208,128]{1,0:T(8,128)(2,1)S(1)}, u32[]{:S(2)}, u32[]{:S(2)}) %collective-permute-start.7) | collective-permute-done | bytes 53280 | tf_op jit(solution)/shard_map/ppermute | solution.py:246
  18.1 0.1 collective-permute-start.9
  18.3 0.0 collective-permute-done.6.refs_4_
  18.3 0.4 %collective-permute-start.8 = (bf16[208,128]{1,0:T(8,128)(2,1)S(1)}, bf16[208,128]{1,0:T(8,128)(2,1)S(1)}, u32[]{:S(2)}, u32[]{:S(2)}) collective-permute-start(bf16[208,128]{1,0:T(8,128)(2,1)S(1)} %collective-permute-done.6.refs_4_), channel_id=1, source_target_pairs={{0,4},{1,5},{2,6},{3,7},{4,0},{5,1},{6,2},{7,3},{8,12},{9,13},{10,... | collective-permute-start | bytes 159752 | tf_op jit(solution)/shard_map/ppermute | solution.py:246
  18.7 0.0 collective-permute-done.3.refs_1_
  18.7 0.0 collective-permute-done.5.refs_3_
  18.7 0.2 shard_map.52.refs_0_
  18.8 0.5 %collective-permute-done.9.refs_2_ = bf16[208,128]{1,0:T(8,128)(2,1)S(1)} collective-permute-done((bf16[208,128]{1,0:T(8,128)(2,1)S(1)}, bf16[208,128]{1,0:T(8,128)(2,1)S(1)}, u32[]{:S(2)}, u32[]{:S(2)}) %collective-permute-start.9) | collective-permute-done | bytes 53280 | tf_op jit(solution)/shard_map/ppermute | solution.py:246
  19.4 0.2 collective-permute-done.8.refs_1_
  19.5 1.8 %shard_map.53 = (f32[32,100]{1,0:T(8,128)}, f32[100,32,100]{2,1,0:T(8,128)}, f32[8,32,8,128]{3,2,1,0:T(8,128)S(1)}) custom-call(f32[8,32,8,128]{3,2,1,0:T(8,128)S(1)} %shard_map.52.refs_0_, bf16[208,128]{1,0:T(8,128)(2,1)S(1)} %collective-permute-done.8.refs_1_, bf16[208,128]{1,0:T(8,128)(2,1)S(1)} %collective-permute-done.9.refs_2_), custom_call_target="tpu_custom_call", output_to_operand_aliasing={{2}: (0, {})} | custom-call | tf_op jit(solution)/shard_map/pallas_call | solution.py:302
Async XLA Ops:
  2.4 5.4 %collective-permute-start = (bf16[128,128]{1,0:T(8,128)(2,1)S(1)}, bf16[128,128]{1,0:T(8,128)(2,1)S(1)}, u32[]{:S(2)}, u32[]{:S(2)}) collective-permute-start(bf16[128,128]{1,0:T(8,128)(2,1)S(1)} %get-tuple-element.8.refs_0_), channel_id=1, source_target_pairs={{0,20},{1,21},{2,22},{3,23},{4,16},{5,17},{6,18},{7,19},{8,28},{9,... | collective-permute-start | bytes 98312 | tf_op jit(solution)/shard_map/ppermute | solution.py:246
  6.0 5.2 %collective-permute-start.2 = (bf16[128,128]{1,0:T(8,128)(2,1)S(1)}, bf16[128,128]{1,0:T(8,128)(2,1)S(1)}, u32[]{:S(2)}, u32[]{:S(2)}) collective-permute-start(bf16[128,128]{1,0:T(8,128)(2,1)S(1)} %get-tuple-element.9), channel_id=1, source_target_pairs={{0,21},{1,20},{2,23},{3,22},{4,17},{5,16},{6,19},{7,18},{8,29},{9,... | collective-permute-start | bytes 98312 | tf_op jit(solution)/shard_map/ppermute | solution.py:246
  7.5 3.7 %collective-permute-start.1 = (bf16[128,128]{1,0:T(8,128)(2,1)S(1)}, bf16[128,128]{1,0:T(8,128)(2,1)S(1)}, u32[]{:S(2)}, u32[]{:S(2)}) collective-permute-start(bf16[128,128]{1,0:T(8,128)(2,1)S(1)} %get-tuple-element.9), channel_id=1, source_target_pairs={{0,5},{1,4},{2,7},{3,6},{4,1},{5,0},{6,3},{7,2},{8,13},{9,12},{10,... | collective-permute-start | bytes 98312 | tf_op jit(solution)/shard_map/ppermute | solution.py:246
  11.4 4.7 %collective-permute-start.4 = (bf16[208,128]{1,0:T(8,128)(2,1)S(1)}, bf16[208,128]{1,0:T(8,128)(2,1)S(1)}, u32[]{:S(2)}, u32[]{:S(2)}) collective-permute-start(bf16[208,128]{1,0:T(8,128)(2,1)S(1)} %get-tuple-element.11), channel_id=1, source_target_pairs={{0,14},{1,15},{2,12},{3,13},{4,10},{5,11},{6,8},{7,9},{8,6},{9,7},... | collective-permute-start | bytes 159752 | tf_op jit(solution)/shard_map/ppermute | solution.py:246
  14.2 4.0 %collective-permute-start.7 = (bf16[208,128]{1,0:T(8,128)(2,1)S(1)}, bf16[208,128]{1,0:T(8,128)(2,1)S(1)}, u32[]{:S(2)}, u32[]{:S(2)}) collective-permute-start(bf16[208,128]{1,0:T(8,128)(2,1)S(1)} %get-tuple-element.11), channel_id=1, source_target_pairs={{0,6},{1,7},{2,4},{3,5},{4,2},{5,3},{6,0},{7,1},{8,14},{9,15},{10,... | collective-permute-start | bytes 159752 | tf_op jit(solution)/shard_map/ppermute | solution.py:246
  14.2 4.0 %collective-permute-start.6 = (bf16[208,128]{1,0:T(8,128)(2,1)S(1)}, bf16[208,128]{1,0:T(8,128)(2,1)S(1)}, u32[]{:S(2)}, u32[]{:S(2)}) collective-permute-start(bf16[208,128]{1,0:T(8,128)(2,1)S(1)} %get-tuple-element.10.refs_0_), channel_id=1, source_target_pairs={{0,12},{1,13},{2,14},{3,15},{4,8},{5,9},{6,10},{7,11},{8,4},{9,5},... | collective-permute-start | bytes 159752 | tf_op jit(solution)/shard_map/ppermute | solution.py:246
  15.2 3.5 %collective-permute-start.3 = (bf16[208,128]{1,0:T(8,128)(2,1)S(1)}, bf16[208,128]{1,0:T(8,128)(2,1)S(1)}, u32[]{:S(2)}, u32[]{:S(2)}) collective-permute-start(bf16[208,128]{1,0:T(8,128)(2,1)S(1)} %get-tuple-element.10.refs_0_), channel_id=1, source_target_pairs={{0,4},{1,5},{2,6},{3,7},{4,0},{5,1},{6,2},{7,3},{8,12},{9,13},{10,... | collective-permute-start | bytes 159752 | tf_op jit(solution)/shard_map/ppermute | solution.py:246
  16.2 2.5 %collective-permute-start.5 = (bf16[208,128]{1,0:T(8,128)(2,1)S(1)}, bf16[208,128]{1,0:T(8,128)(2,1)S(1)}, u32[]{:S(2)}, u32[]{:S(2)}) collective-permute-start(bf16[208,128]{1,0:T(8,128)(2,1)S(1)} %collective-permute-done.4.refs_2_), channel_id=1, source_target_pairs={{0,4},{1,5},{2,6},{3,7},{4,0},{5,1},{6,2},{7,3},{8,12},{9,13},{10,... | collective-permute-start | bytes 159752 | tf_op jit(solution)/shard_map/ppermute | solution.py:246
  18.1 1.2 %collective-permute-start.9 = (bf16[208,128]{1,0:T(8,128)(2,1)S(1)}, bf16[208,128]{1,0:T(8,128)(2,1)S(1)}, u32[]{:S(2)}, u32[]{:S(2)}) collective-permute-start(bf16[208,128]{1,0:T(8,128)(2,1)S(1)} %collective-permute-done.7.refs_5_), channel_id=1, source_target_pairs={{0,4},{1,5},{2,6},{3,7},{4,0},{5,1},{6,2},{7,3},{8,12},{9,13},{10,... | collective-permute-start | bytes 159752 | tf_op jit(solution)/shard_map/ppermute | solution.py:246
  18.3 1.3 %collective-permute-start.8 = (bf16[208,128]{1,0:T(8,128)(2,1)S(1)}, bf16[208,128]{1,0:T(8,128)(2,1)S(1)}, u32[]{:S(2)}, u32[]{:S(2)}) collective-permute-start(bf16[208,128]{1,0:T(8,128)(2,1)S(1)} %collective-permute-done.6.refs_4_), channel_id=1, source_target_pairs={{0,4},{1,5},{2,6},{3,7},{4,0},{5,1},{6,2},{7,3},{8,12},{9,13},{10,... | collective-permute-start | bytes 159752 | tf_op jit(solution)/shard_map/ppermute | solution.py:246

commit v7 on v5

--- a/solution.py
+++ b/solution.py
@@ -22,14 +22,15 @@
     return pos_dev - extra, extra
 
 
-def unpack(ref, images, pos_dev):
-    block = ref[...].astype(jnp.float32)
-    size = packing(pos_dev)[1] * images
+def unpack(ref, images, pos_dev, part=0):
+    base, extra = packing(pos_dev)
+    block = ref[pl.ds(part * base * images, base * images), :].astype(jnp.float32)
+    size = extra * images
     place = lax.broadcasted_iota(jnp.int32, (size, LANES), 1) // PIECE
     moved = None
     for piece in range(PIECES):
-        part = pltpu.roll(block[piece * size : (piece + 1) * size], LANES - CH + piece * PIECE, 1)
-        moved = part if moved is None else jnp.where(place == piece, part, moved)
+        turned = pltpu.roll(block[piece * size : (piece + 1) * size], LANES - CH + piece * PIECE, 1)
+        moved = turned if moved is None else jnp.where(place == piece, turned, moved)
     return jnp.concatenate([block, moved], axis=0).reshape(pos_dev, images, LANES)
 
 
@@ -141,20 +142,20 @@
     *in_refs, held = refs
     kept, where = places(dims, images)
     for i, step in enumerate(whole):
-        first, second = (unpack(in_refs[CORES * i + j], images, pos_dev) for j in range(CORES))
-        put(held, kept, where[step], first, second)
+        first = unpack(in_refs[i], images, pos_dev)
+        put(held, kept, where[step], first, unpack(in_refs[-1], images, pos_dev, i))
     for i, step in enumerate(half):
-        held[where[step][0]] = unpack(in_refs[CORES * len(whole) + i], images, pos_dev)
+        held[where[step][0]] = unpack(in_refs[len(whole) + i], images, pos_dev)
 
 
 def stats_kernel(dims, images, pos_dev, half, *refs):
     z_low, z_high, pos_low, pos_high = dims
     blocks = pos_high * z_low * CORES
-    _, *in_refs = refs[: 1 + len(half)]
-    mean_hbm, cov_hbm, held, mean_ref, cov_ref, turn_ref, sems = refs[1 + len(half) :]
+    _, in_ref, mean_hbm, cov_hbm, held, mean_ref, cov_ref, turn_ref, sems = refs
     kept, where = places(dims, images)
-    for step, ref in zip(half, in_refs):
-        put(held, kept, where[step], held[where[step][0]], unpack(ref, images, pos_dev))
+    for i, step in enumerate(half):
+        second = unpack(in_ref, images, pos_dev, i)
+        put(held, kept, where[step], held[where[step][0]], second)
     base = packing(pos_dev)[0]
     everyone = blocks * images
     live = jnp.broadcast_to(
@@ -268,13 +269,13 @@
     near = {(0, 0): owns[0]}
     for step in far_first(pos_high, z_low):
         near[step] = send(owns[step[0]], pos_high_step=step[0], z_low_step=step[1], core_step=1)
-    other = {step: send(near[step], core_step=1) for step in near}
     steps = [(0, 0), *far_first(pos_high, z_low)]
     count = max(1, len(steps) // 2)
     whole, half = steps[:count], steps[count:]
+    early_other = send(jnp.concatenate([near[step] for step in whole], axis=0), core_step=1)
+    late = send(jnp.concatenate([near[step] for step in half], axis=0), core_step=1)
     held = jax.ShapeDtypeStruct((pos_high * z_low * CORES, pos_dev, images, LANES), jnp.float32)
-    early = [block for step in whole for block in (near[step], other[step])]
-    early += [near[step] for step in half]
+    early = [near[step] for step in (*whole, *half)] + [early_other]
     ready = pl.pallas_call(
         functools.partial(prepare_kernel, dims, images, pos_dev, whole, half),
         out_shape=held,
@@ -294,7 +295,7 @@
             jax.ShapeDtypeStruct((CH, pos_dev, CH), jnp.float32),
             held,
         ],
-        in_specs=[vmem] * (1 + len(half)),
+        in_specs=[vmem, vmem],
         out_specs=[hbm, hbm, vmem],
         input_output_aliases={0: 2},
         scratch_shapes=[
@@ -304,7 +305,7 @@
             pltpu.SemaphoreType.DMA((pos_dev // ROWS + 1,)),
         ],
         compiler_params=pltpu.CompilerParams(vmem_limit_bytes=32 * MIB),
-    )(ready, *(other[step] for step in half))
+    )(ready, late)
     return mean, jnp.transpose(covariance, (1, 0, 2))
 
 

time: 21.5 us -> 21.5 us (level)
    ppermute x10 -> x8, starting transfers between devices: 10.3 us -> 10.2 us  [send(): return lax.ppermute(block, ('dp', 'pos'), pairs)]
    ppermute x10 -> x8, waiting for transfers between devices: 6.42 us -> 6.57 us  [send(): return lax.ppermute(block, ('dp', 'pos'), pairs)]
  transfers between devices with their start and end apart: 10 -> 8, of which waited for: 5 -> 4; matrix products, arithmetic and copies ran while one was open for 0% -> 0% of each run, Pallas kernels for 1% -> 1%
where the time goes in v7:
time: 21.5 us; the launch traced here: 21.3 us
  starting transfers between devices  10.2 us (47%)
  waiting for transfers between devices  6.57 us (31%)
  Pallas kernels  3.25 us (15%)
  between operations  1.31 us (6%)
    ppermute x8, starting transfers between devices, send(): return lax.ppermute(block, ('dp', 'pos'), pairs)  10.2 us
    ppermute x8, waiting for transfers between devices, send(): return lax.ppermute(block, ('dp', 'pos'), pairs)  6.57 us
    pallas_call x1, Pallas kernels, on_device(): pl.pallas_call(functools.partial(stats_kernel, dims, images, pos_dev, hal...  1.78 us
    pallas_call x1, Pallas kernels, on_device(): pl.pallas_call(functools.partial(select_kernel, (pos_low, pos_high), pos_...  1.17 us
  transfers between devices with their start and end apart: 8, of which 4 were waited for; matrix products, arithmetic and copies ran while one was open for 0% of the time, Pallas kernels for 1%

profile of v7, /device:TPU:0, one launch (start us, length us, event | category | flops | bytes accessed | tf_op | source)
XLA Modules:
  0.0 21.3 jit_solution(12887184705711841817)
XLA Ops:
  1.3 1.2 %shard_map.50 = (bf16[128,128]{1,0:T(8,128)(2,1)S(1)}, bf16[128,128]{1,0:T(8,128)(2,1)S(1)}) custom-call(bf16[2,224,128]{2,1,0:T(8,128)(2,1)} %bitcast.2, s32[1]{0:T(128)S(6)} %copy.7.counts_ref, s32[224]{0:T(256)} %order_hbm.1), custom_call_target="tpu_custom_call" | custom-call | tf_op jit(solution)/shard_map/pallas_call | solution.py:238
  2.4 3.5 %collective-permute-start = (bf16[128,128]{1,0:T(8,128)(2,1)S(1)}, bf16[128,128]{1,0:T(8,128)(2,1)S(1)}, u32[]{:S(2)}, u32[]{:S(2)}) collective-permute-start(bf16[128,128]{1,0:T(8,128)(2,1)S(1)} %get-tuple-element.8.refs_0_), channel_id=1, source_target_pairs={{0,20},{1,21},{2,22},{3,23},{4,16},{5,17},{6,18},{7,19},{8,28},{9,... | collective-permute-start | bytes 98312 | tf_op jit(solution)/shard_map/ppermute | solution.py:235
  6.0 1.5 %collective-permute-start.2 = (bf16[128,128]{1,0:T(8,128)(2,1)S(1)}, bf16[128,128]{1,0:T(8,128)(2,1)S(1)}, u32[]{:S(2)}, u32[]{:S(2)}) collective-permute-start(bf16[128,128]{1,0:T(8,128)(2,1)S(1)} %get-tuple-element.9), channel_id=1, source_target_pairs={{0,21},{1,20},{2,23},{3,22},{4,17},{5,16},{6,19},{7,18},{8,29},{9,... | collective-permute-start | bytes 98312 | tf_op jit(solution)/shard_map/ppermute | solution.py:235
  7.5 0.3 %collective-permute-start.1 = (bf16[128,128]{1,0:T(8,128)(2,1)S(1)}, bf16[128,128]{1,0:T(8,128)(2,1)S(1)}, u32[]{:S(2)}, u32[]{:S(2)}) collective-permute-start(bf16[128,128]{1,0:T(8,128)(2,1)S(1)} %get-tuple-element.9), channel_id=1, source_target_pairs={{0,5},{1,4},{2,7},{3,6},{4,1},{5,0},{6,3},{7,2},{8,13},{9,12},{10,... | collective-permute-start | bytes 98312 | tf_op jit(solution)/shard_map/ppermute | solution.py:235
  7.8 0.0 collective-permute-done.refs_1_
  7.8 3.4 %collective-permute-done.2.refs_3_ = bf16[128,128]{1,0:T(8,128)(2,1)S(1)} collective-permute-done((bf16[128,128]{1,0:T(8,128)(2,1)S(1)}, bf16[128,128]{1,0:T(8,128)(2,1)S(1)}, u32[]{:S(2)}, u32[]{:S(2)}) %collective-permute-start.2) | collective-permute-done | bytes 32800 | tf_op jit(solution)/shard_map/ppermute | solution.py:235
  11.2 0.0 collective-permute-done.1.refs_2_
  11.3 0.1 shard_map.51
  11.4 2.8 %collective-permute-start.3 = (bf16[208,128]{1,0:T(8,128)(2,1)S(1)}, bf16[208,128]{1,0:T(8,128)(2,1)S(1)}, u32[]{:S(2)}, u32[]{:S(2)}) collective-permute-start(bf16[208,128]{1,0:T(8,128)(2,1)S(1)} %get-tuple-element.11), channel_id=1, source_target_pairs={{0,14},{1,15},{2,12},{3,13},{4,10},{5,11},{6,8},{7,9},{8,6},{9,7},... | collective-permute-start | bytes 159752 | tf_op jit(solution)/shard_map/ppermute | solution.py:235
  14.2 0.1 collective-permute-start.5
  14.2 0.9 %collective-permute-start.4 = (bf16[208,128]{1,0:T(8,128)(2,1)S(1)}, bf16[208,128]{1,0:T(8,128)(2,1)S(1)}, u32[]{:S(2)}, u32[]{:S(2)}) collective-permute-start(bf16[208,128]{1,0:T(8,128)(2,1)S(1)} %get-tuple-element.10.refs_0_), channel_id=1, source_target_pairs={{0,12},{1,13},{2,14},{3,15},{4,8},{5,9},{6,10},{7,11},{8,4},{9,5},... | collective-permute-start | bytes 159752 | tf_op jit(solution)/shard_map/ppermute | solution.py:235
  15.2 1.0 %collective-permute-done.3.refs_1_ = bf16[208,128]{1,0:T(8,128)(2,1)S(1)} collective-permute-done((bf16[208,128]{1,0:T(8,128)(2,1)S(1)}, bf16[208,128]{1,0:T(8,128)(2,1)S(1)}, u32[]{:S(2)}, u32[]{:S(2)}) %collective-permute-start.3) | collective-permute-done | bytes 53280 | tf_op jit(solution)/shard_map/ppermute | solution.py:235
  16.2 0.7 %collective-permute-start.6 = (bf16[416,128]{1,0:T(8,128)(2,1)S(1)}, bf16[416,128]{1,0:T(8,128)(2,1)S(1)}, u32[]{:S(2)}, u32[]{:S(2)}) collective-permute-start(bf16[416,128]{1,0:T(8,128)(2,1)S(1)} %pad_maximum_fusion), channel_id=1, source_target_pairs={{0,4},{1,5},{2,6},{3,7},{4,0},{5,1},{6,2},{7,3},{8,12},{9,13},{10,... | collective-permute-start | bytes 319496 | tf_op jit(solution)/shard_map/ppermute | solution.py:235
  16.9 1.2 %collective-permute-done.5.refs_3_ = bf16[208,128]{1,0:T(8,128)(2,1)S(1)} collective-permute-done((bf16[208,128]{1,0:T(8,128)(2,1)S(1)}, bf16[208,128]{1,0:T(8,128)(2,1)S(1)}, u32[]{:S(2)}, u32[]{:S(2)}) %collective-permute-start.5) | collective-permute-done | bytes 53280 | tf_op jit(solution)/shard_map/ppermute | solution.py:235
  18.1 0.0 collective-permute-done.4.refs_2_
  18.2 0.3 %collective-permute-start.7 = (bf16[416,128]{1,0:T(8,128)(2,1)S(1)}, bf16[416,128]{1,0:T(8,128)(2,1)S(1)}, u32[]{:S(2)}, u32[]{:S(2)}) collective-permute-start(bf16[416,128]{1,0:T(8,128)(2,1)S(1)} %pad_maximum_fusion.1), channel_id=1, source_target_pairs={{0,4},{1,5},{2,6},{3,7},{4,0},{5,1},{6,2},{7,3},{8,12},{9,13},{10,... | collective-permute-start | bytes 319496 | tf_op jit(solution)/shard_map/ppermute | solution.py:235
  18.4 0.0 collective-permute-done.6.refs_4_
  18.4 0.2 shard_map.52.refs_0_
  18.6 0.9 %collective-permute-done.7.refs_1_ = bf16[416,128]{1,0:T(8,128)(2,1)S(1)} collective-permute-done((bf16[416,128]{1,0:T(8,128)(2,1)S(1)}, bf16[416,128]{1,0:T(8,128)(2,1)S(1)}, u32[]{:S(2)}, u32[]{:S(2)}) %collective-permute-start.7) | collective-permute-done | bytes 106528 | tf_op jit(solution)/shard_map/ppermute | solution.py:235
  19.5 1.8 %shard_map.53 = (f32[32,100]{1,0:T(8,128)}, f32[100,32,100]{2,1,0:T(8,128)}, f32[8,32,8,128]{3,2,1,0:T(8,128)S(1)}) custom-call(f32[8,32,8,128]{3,2,1,0:T(8,128)S(1)} %shard_map.52.refs_0_, bf16[416,128]{1,0:T(8,128)(2,1)S(1)} %collective-permute-done.7.refs_1_), custom_call_target="tpu_custom_call", output_to_operand_aliasing={{2}: (0, {})} | custom-call | tf_op jit(solution)/shard_map/pallas_call | solution.py:291
  (2 shorter events, 0.0 us)
Async XLA Ops:
  2.4 5.4 %collective-permute-start = (bf16[128,128]{1,0:T(8,128)(2,1)S(1)}, bf16[128,128]{1,0:T(8,128)(2,1)S(1)}, u32[]{:S(2)}, u32[]{:S(2)}) collective-permute-start(bf16[128,128]{1,0:T(8,128)(2,1)S(1)} %get-tuple-element.8.refs_0_), channel_id=1, source_target_pairs={{0,20},{1,21},{2,22},{3,23},{4,16},{5,17},{6,18},{7,19},{8,28},{9,... | collective-permute-start | bytes 98312 | tf_op jit(solution)/shard_map/ppermute | solution.py:235
  6.0 5.2 %collective-permute-start.2 = (bf16[128,128]{1,0:T(8,128)(2,1)S(1)}, bf16[128,128]{1,0:T(8,128)(2,1)S(1)}, u32[]{:S(2)}, u32[]{:S(2)}) collective-permute-start(bf16[128,128]{1,0:T(8,128)(2,1)S(1)} %get-tuple-element.9), channel_id=1, source_target_pairs={{0,21},{1,20},{2,23},{3,22},{4,17},{5,16},{6,19},{7,18},{8,29},{9,... | collective-permute-start | bytes 98312 | tf_op jit(solution)/shard_map/ppermute | solution.py:235
  7.5 3.7 %collective-permute-start.1 = (bf16[128,128]{1,0:T(8,128)(2,1)S(1)}, bf16[128,128]{1,0:T(8,128)(2,1)S(1)}, u32[]{:S(2)}, u32[]{:S(2)}) collective-permute-start(bf16[128,128]{1,0:T(8,128)(2,1)S(1)} %get-tuple-element.9), channel_id=1, source_target_pairs={{0,5},{1,4},{2,7},{3,6},{4,1},{5,0},{6,3},{7,2},{8,13},{9,12},{10,... | collective-permute-start | bytes 98312 | tf_op jit(solution)/shard_map/ppermute | solution.py:235
  11.4 4.7 %collective-permute-start.3 = (bf16[208,128]{1,0:T(8,128)(2,1)S(1)}, bf16[208,128]{1,0:T(8,128)(2,1)S(1)}, u32[]{:S(2)}, u32[]{:S(2)}) collective-permute-start(bf16[208,128]{1,0:T(8,128)(2,1)S(1)} %get-tuple-element.11), channel_id=1, source_target_pairs={{0,14},{1,15},{2,12},{3,13},{4,10},{5,11},{6,8},{7,9},{8,6},{9,7},... | collective-permute-start | bytes 159752 | tf_op jit(solution)/shard_map/ppermute | solution.py:235
  14.2 4.0 %collective-permute-start.5 = (bf16[208,128]{1,0:T(8,128)(2,1)S(1)}, bf16[208,128]{1,0:T(8,128)(2,1)S(1)}, u32[]{:S(2)}, u32[]{:S(2)}) collective-permute-start(bf16[208,128]{1,0:T(8,128)(2,1)S(1)} %get-tuple-element.11), channel_id=1, source_target_pairs={{0,6},{1,7},{2,4},{3,5},{4,2},{5,3},{6,0},{7,1},{8,14},{9,15},{10,... | collective-permute-start | bytes 159752 | tf_op jit(solution)/shard_map/ppermute | solution.py:235
  14.2 3.9 %collective-permute-start.4 = (bf16[208,128]{1,0:T(8,128)(2,1)S(1)}, bf16[208,128]{1,0:T(8,128)(2,1)S(1)}, u32[]{:S(2)}, u32[]{:S(2)}) collective-permute-start(bf16[208,128]{1,0:T(8,128)(2,1)S(1)} %get-tuple-element.10.refs_0_), channel_id=1, source_target_pairs={{0,12},{1,13},{2,14},{3,15},{4,8},{5,9},{6,10},{7,11},{8,4},{9,5},... | collective-permute-start | bytes 159752 | tf_op jit(solution)/shard_map/ppermute | solution.py:235
  16.2 2.3 %collective-permute-start.6 = (bf16[416,128]{1,0:T(8,128)(2,1)S(1)}, bf16[416,128]{1,0:T(8,128)(2,1)S(1)}, u32[]{:S(2)}, u32[]{:S(2)}) collective-permute-start(bf16[416,128]{1,0:T(8,128)(2,1)S(1)} %pad_maximum_fusion), channel_id=1, source_target_pairs={{0,4},{1,5},{2,6},{3,7},{4,0},{5,1},{6,2},{7,3},{8,12},{9,13},{10,... | collective-permute-start | bytes 319496 | tf_op jit(solution)/shard_map/ppermute | solution.py:235
  18.2 1.4 %collective-permute-start.7 = (bf16[416,128]{1,0:T(8,128)(2,1)S(1)}, bf16[416,128]{1,0:T(8,128)(2,1)S(1)}, u32[]{:S(2)}, u32[]{:S(2)}) collective-permute-start(bf16[416,128]{1,0:T(8,128)(2,1)S(1)} %pad_maximum_fusion.1), channel_id=1, source_target_pairs={{0,4},{1,5},{2,6},{3,7},{4,0},{5,1},{6,2},{7,3},{8,12},{9,13},{10,... | collective-permute-start | bytes 319496 | tf_op jit(solution)/shard_map/ppermute | solution.py:235

commit v8 on v5

--- a/solution.py
+++ b/solution.py
@@ -177,6 +177,7 @@
         )
 
     def one_group(group, _):
+        tiles = []
         for row in range(ROWS):
             position = group * ROWS + row
             samples = held[:, position].reshape(everyone, LANES)
@@ -192,9 +193,8 @@
                 (((1,), (0,)), ((), ())),
                 preferred_element_type=jnp.float32,
             )
-            turn_ref[group, pl.ds(row, tall, stride=PITCH), :] = sums * factor + ridge
-        for channel in range(CH):
-            cov_ref[group, channel] = turn_ref[group, pl.ds(channel * PITCH, ROWS), :CH]
+            tiles.append(sums * factor + ridge)
+        cov_ref[group] = jnp.swapaxes(jnp.stack(tiles), 0, 1)[:CH, :, :CH]
         out(group).start()
         return 0
 

time: 21.5 us -> 21.5 us (level)
  no operation moved by 1% of the time
where the time goes in v8:
time: 21.5 us; the launch traced here: 21.3 us
  starting transfers between devices  10.3 us (48%)
  waiting for transfers between devices  6.42 us (30%)
  Pallas kernels  3.26 us (15%)
  between operations  1.31 us (6%)
    ppermute x10, starting transfers between devices, send(): return lax.ppermute(block, ('dp', 'pos'), pairs)  10.3 us
    ppermute x10, waiting for transfers between devices, send(): return lax.ppermute(block, ('dp', 'pos'), pairs)  6.42 us
    pallas_call x1, Pallas kernels, on_device(): pl.pallas_call(functools.partial(stats_kernel, dims, images, pos_dev, hal...  1.79 us
    pallas_call x1, Pallas kernels, on_device(): pl.pallas_call(functools.partial(select_kernel, (pos_low, pos_high), pos_...  1.17 us
  transfers between devices with their start and end apart: 10, of which 5 were waited for; matrix products, arithmetic and copies ran while one was open for 0% of the time, Pallas kernels for 1%

profile of v8, /device:TPU:0, one launch (start us, length us, event | category | flops | bytes accessed | tf_op | source)
XLA Modules:
  0.0 21.3 jit_solution(13427962538318989019)
XLA Ops:
  1.3 1.2 %shard_map.50 = (bf16[128,128]{1,0:T(8,128)(2,1)S(1)}, bf16[128,128]{1,0:T(8,128)(2,1)S(1)}) custom-call(bf16[2,224,128]{2,1,0:T(8,128)(2,1)} %bitcast.2, s32[1]{0:T(128)S(6)} %copy.7.counts_ref, s32[224]{0:T(256)} %order_hbm.1), custom_call_target="tpu_custom_call" | custom-call | tf_op jit(solution)/shard_map/pallas_call | solution.py:237
  2.4 3.5 %collective-permute-start = (bf16[128,128]{1,0:T(8,128)(2,1)S(1)}, bf16[128,128]{1,0:T(8,128)(2,1)S(1)}, u32[]{:S(2)}, u32[]{:S(2)}) collective-permute-start(bf16[128,128]{1,0:T(8,128)(2,1)S(1)} %get-tuple-element.8.refs_0_), channel_id=1, source_target_pairs={{0,20},{1,21},{2,22},{3,23},{4,16},{5,17},{6,18},{7,19},{8,28},{9,... | collective-permute-start | bytes 98312 | tf_op jit(solution)/shard_map/ppermute | solution.py:234
  6.0 1.5 %collective-permute-start.2 = (bf16[128,128]{1,0:T(8,128)(2,1)S(1)}, bf16[128,128]{1,0:T(8,128)(2,1)S(1)}, u32[]{:S(2)}, u32[]{:S(2)}) collective-permute-start(bf16[128,128]{1,0:T(8,128)(2,1)S(1)} %get-tuple-element.9), channel_id=1, source_target_pairs={{0,21},{1,20},{2,23},{3,22},{4,17},{5,16},{6,19},{7,18},{8,29},{9,... | collective-permute-start | bytes 98312 | tf_op jit(solution)/shard_map/ppermute | solution.py:234
  7.5 0.3 %collective-permute-start.1 = (bf16[128,128]{1,0:T(8,128)(2,1)S(1)}, bf16[128,128]{1,0:T(8,128)(2,1)S(1)}, u32[]{:S(2)}, u32[]{:S(2)}) collective-permute-start(bf16[128,128]{1,0:T(8,128)(2,1)S(1)} %get-tuple-element.9), channel_id=1, source_target_pairs={{0,5},{1,4},{2,7},{3,6},{4,1},{5,0},{6,3},{7,2},{8,13},{9,12},{10,... | collective-permute-start | bytes 98312 | tf_op jit(solution)/shard_map/ppermute | solution.py:234
  7.8 0.0 collective-permute-done.refs_1_
  7.8 3.4 %collective-permute-done.2.refs_3_ = bf16[128,128]{1,0:T(8,128)(2,1)S(1)} collective-permute-done((bf16[128,128]{1,0:T(8,128)(2,1)S(1)}, bf16[128,128]{1,0:T(8,128)(2,1)S(1)}, u32[]{:S(2)}, u32[]{:S(2)}) %collective-permute-start.2) | collective-permute-done | bytes 32800 | tf_op jit(solution)/shard_map/ppermute | solution.py:234
  11.2 0.0 collective-permute-done.1.refs_2_
  11.3 0.1 shard_map.51
  11.4 2.8 %collective-permute-start.4 = (bf16[208,128]{1,0:T(8,128)(2,1)S(1)}, bf16[208,128]{1,0:T(8,128)(2,1)S(1)}, u32[]{:S(2)}, u32[]{:S(2)}) collective-permute-start(bf16[208,128]{1,0:T(8,128)(2,1)S(1)} %get-tuple-element.11), channel_id=1, source_target_pairs={{0,14},{1,15},{2,12},{3,13},{4,10},{5,11},{6,8},{7,9},{8,6},{9,7},... | collective-permute-start | bytes 159752 | tf_op jit(solution)/shard_map/ppermute | solution.py:234
  14.2 0.1 collective-permute-start.7
  14.2 0.9 %collective-permute-start.6 = (bf16[208,128]{1,0:T(8,128)(2,1)S(1)}, bf16[208,128]{1,0:T(8,128)(2,1)S(1)}, u32[]{:S(2)}, u32[]{:S(2)}) collective-permute-start(bf16[208,128]{1,0:T(8,128)(2,1)S(1)} %get-tuple-element.10.refs_0_), channel_id=1, source_target_pairs={{0,12},{1,13},{2,14},{3,15},{4,8},{5,9},{6,10},{7,11},{8,4},{9,5},... | collective-permute-start | bytes 159752 | tf_op jit(solution)/shard_map/ppermute | solution.py:234
  15.2 0.0 collective-permute-start.3
  15.2 1.0 %collective-permute-done.4.refs_2_ = bf16[208,128]{1,0:T(8,128)(2,1)S(1)} collective-permute-done((bf16[208,128]{1,0:T(8,128)(2,1)S(1)}, bf16[208,128]{1,0:T(8,128)(2,1)S(1)}, u32[]{:S(2)}, u32[]{:S(2)}) %collective-permute-start.4) | collective-permute-done | bytes 53280 | tf_op jit(solution)/shard_map/ppermute | solution.py:234
  16.2 0.7 %collective-permute-start.5 = (bf16[208,128]{1,0:T(8,128)(2,1)S(1)}, bf16[208,128]{1,0:T(8,128)(2,1)S(1)}, u32[]{:S(2)}, u32[]{:S(2)}) collective-permute-start(bf16[208,128]{1,0:T(8,128)(2,1)S(1)} %collective-permute-done.4.refs_2_), channel_id=1, source_target_pairs={{0,4},{1,5},{2,6},{3,7},{4,0},{5,1},{6,2},{7,3},{8,12},{9,13},{10,... | collective-permute-start | bytes 159752 | tf_op jit(solution)/shard_map/ppermute | solution.py:234
  16.8 1.3 %collective-permute-done.7.refs_5_ = bf16[208,128]{1,0:T(8,128)(2,1)S(1)} collective-permute-done((bf16[208,128]{1,0:T(8,128)(2,1)S(1)}, bf16[208,128]{1,0:T(8,128)(2,1)S(1)}, u32[]{:S(2)}, u32[]{:S(2)}) %collective-permute-start.7) | collective-permute-done | bytes 53280 | tf_op jit(solution)/shard_map/ppermute | solution.py:234
  18.1 0.1 collective-permute-start.9
  18.3 0.0 collective-permute-done.6.refs_4_
  18.3 0.4 %collective-permute-start.8 = (bf16[208,128]{1,0:T(8,128)(2,1)S(1)}, bf16[208,128]{1,0:T(8,128)(2,1)S(1)}, u32[]{:S(2)}, u32[]{:S(2)}) collective-permute-start(bf16[208,128]{1,0:T(8,128)(2,1)S(1)} %collective-permute-done.6.refs_4_), channel_id=1, source_target_pairs={{0,4},{1,5},{2,6},{3,7},{4,0},{5,1},{6,2},{7,3},{8,12},{9,13},{10,... | collective-permute-start | bytes 159752 | tf_op jit(solution)/shard_map/ppermute | solution.py:234
  18.7 0.0 collective-permute-done.3.refs_1_
  18.7 0.0 collective-permute-done.5.refs_3_
  18.7 0.2 shard_map.52.refs_0_
  18.8 0.5 %collective-permute-done.9.refs_2_ = bf16[208,128]{1,0:T(8,128)(2,1)S(1)} collective-permute-done((bf16[208,128]{1,0:T(8,128)(2,1)S(1)}, bf16[208,128]{1,0:T(8,128)(2,1)S(1)}, u32[]{:S(2)}, u32[]{:S(2)}) %collective-permute-start.9) | collective-permute-done | bytes 53280 | tf_op jit(solution)/shard_map/ppermute | solution.py:234
  19.4 0.2 collective-permute-done.8.refs_1_
  19.5 1.8 %shard_map.53 = (f32[32,100]{1,0:T(8,128)}, f32[100,32,100]{2,1,0:T(8,128)}, f32[8,32,8,128]{3,2,1,0:T(8,128)S(1)}) custom-call(f32[8,32,8,128]{3,2,1,0:T(8,128)S(1)} %shard_map.52.refs_0_, bf16[208,128]{1,0:T(8,128)(2,1)S(1)} %collective-permute-done.8.refs_1_, bf16[208,128]{1,0:T(8,128)(2,1)S(1)} %collective-permute-done.9.refs_2_), custom_call_target="tpu_custom_call", output_to_operand_aliasing={{2}: (0, {})} | custom-call | tf_op jit(solution)/shard_map/pallas_call | solution.py:290
Async XLA Ops:
  2.4 5.4 %collective-permute-start = (bf16[128,128]{1,0:T(8,128)(2,1)S(1)}, bf16[128,128]{1,0:T(8,128)(2,1)S(1)}, u32[]{:S(2)}, u32[]{:S(2)}) collective-permute-start(bf16[128,128]{1,0:T(8,128)(2,1)S(1)} %get-tuple-element.8.refs_0_), channel_id=1, source_target_pairs={{0,20},{1,21},{2,22},{3,23},{4,16},{5,17},{6,18},{7,19},{8,28},{9,... | collective-permute-start | bytes 98312 | tf_op jit(solution)/shard_map/ppermute | solution.py:234
  6.0 5.2 %collective-permute-start.2 = (bf16[128,128]{1,0:T(8,128)(2,1)S(1)}, bf16[128,128]{1,0:T(8,128)(2,1)S(1)}, u32[]{:S(2)}, u32[]{:S(2)}) collective-permute-start(bf16[128,128]{1,0:T(8,128)(2,1)S(1)} %get-tuple-element.9), channel_id=1, source_target_pairs={{0,21},{1,20},{2,23},{3,22},{4,17},{5,16},{6,19},{7,18},{8,29},{9,... | collective-permute-start | bytes 98312 | tf_op jit(solution)/shard_map/ppermute | solution.py:234
  7.5 3.7 %collective-permute-start.1 = (bf16[128,128]{1,0:T(8,128)(2,1)S(1)}, bf16[128,128]{1,0:T(8,128)(2,1)S(1)}, u32[]{:S(2)}, u32[]{:S(2)}) collective-permute-start(bf16[128,128]{1,0:T(8,128)(2,1)S(1)} %get-tuple-element.9), channel_id=1, source_target_pairs={{0,5},{1,4},{2,7},{3,6},{4,1},{5,0},{6,3},{7,2},{8,13},{9,12},{10,... | collective-permute-start | bytes 98312 | tf_op jit(solution)/shard_map/ppermute | solution.py:234
  11.4 4.7 %collective-permute-start.4 = (bf16[208,128]{1,0:T(8,128)(2,1)S(1)}, bf16[208,128]{1,0:T(8,128)(2,1)S(1)}, u32[]{:S(2)}, u32[]{:S(2)}) collective-permute-start(bf16[208,128]{1,0:T(8,128)(2,1)S(1)} %get-tuple-element.11), channel_id=1, source_target_pairs={{0,14},{1,15},{2,12},{3,13},{4,10},{5,11},{6,8},{7,9},{8,6},{9,7},... | collective-permute-start | bytes 159752 | tf_op jit(solution)/shard_map/ppermute | solution.py:234
  14.2 4.0 %collective-permute-start.7 = (bf16[208,128]{1,0:T(8,128)(2,1)S(1)}, bf16[208,128]{1,0:T(8,128)(2,1)S(1)}, u32[]{:S(2)}, u32[]{:S(2)}) collective-permute-start(bf16[208,128]{1,0:T(8,128)(2,1)S(1)} %get-tuple-element.11), channel_id=1, source_target_pairs={{0,6},{1,7},{2,4},{3,5},{4,2},{5,3},{6,0},{7,1},{8,14},{9,15},{10,... | collective-permute-start | bytes 159752 | tf_op jit(solution)/shard_map/ppermute | solution.py:234
  14.2 4.0 %collective-permute-start.6 = (bf16[208,128]{1,0:T(8,128)(2,1)S(1)}, bf16[208,128]{1,0:T(8,128)(2,1)S(1)}, u32[]{:S(2)}, u32[]{:S(2)}) collective-permute-start(bf16[208,128]{1,0:T(8,128)(2,1)S(1)} %get-tuple-element.10.refs_0_), channel_id=1, source_target_pairs={{0,12},{1,13},{2,14},{3,15},{4,8},{5,9},{6,10},{7,11},{8,4},{9,5},... | collective-permute-start | bytes 159752 | tf_op jit(solution)/shard_map/ppermute | solution.py:234
  15.2 3.5 %collective-permute-start.3 = (bf16[208,128]{1,0:T(8,128)(2,1)S(1)}, bf16[208,128]{1,0:T(8,128)(2,1)S(1)}, u32[]{:S(2)}, u32[]{:S(2)}) collective-permute-start(bf16[208,128]{1,0:T(8,128)(2,1)S(1)} %get-tuple-element.10.refs_0_), channel_id=1, source_target_pairs={{0,4},{1,5},{2,6},{3,7},{4,0},{5,1},{6,2},{7,3},{8,12},{9,13},{10,... | collective-permute-start | bytes 159752 | tf_op jit(solution)/shard_map/ppermute | solution.py:234
  16.2 2.5 %collective-permute-start.5 = (bf16[208,128]{1,0:T(8,128)(2,1)S(1)}, bf16[208,128]{1,0:T(8,128)(2,1)S(1)}, u32[]{:S(2)}, u32[]{:S(2)}) collective-permute-start(bf16[208,128]{1,0:T(8,128)(2,1)S(1)} %collective-permute-done.4.refs_2_), channel_id=1, source_target_pairs={{0,4},{1,5},{2,6},{3,7},{4,0},{5,1},{6,2},{7,3},{8,12},{9,13},{10,... | collective-permute-start | bytes 159752 | tf_op jit(solution)/shard_map/ppermute | solution.py:234
  18.1 1.2 %collective-permute-start.9 = (bf16[208,128]{1,0:T(8,128)(2,1)S(1)}, bf16[208,128]{1,0:T(8,128)(2,1)S(1)}, u32[]{:S(2)}, u32[]{:S(2)}) collective-permute-start(bf16[208,128]{1,0:T(8,128)(2,1)S(1)} %collective-permute-done.7.refs_5_), channel_id=1, source_target_pairs={{0,4},{1,5},{2,6},{3,7},{4,0},{5,1},{6,2},{7,3},{8,12},{9,13},{10,... | collective-permute-start | bytes 159752 | tf_op jit(solution)/shard_map/ppermute | solution.py:234
  18.3 1.3 %collective-permute-start.8 = (bf16[208,128]{1,0:T(8,128)(2,1)S(1)}, bf16[208,128]{1,0:T(8,128)(2,1)S(1)}, u32[]{:S(2)}, u32[]{:S(2)}) collective-permute-start(bf16[208,128]{1,0:T(8,128)(2,1)S(1)} %collective-permute-done.6.refs_4_), channel_id=1, source_target_pairs={{0,4},{1,5},{2,6},{3,7},{4,0},{5,1},{6,2},{7,3},{8,12},{9,13},{10,... | collective-permute-start | bytes 159752 | tf_op jit(solution)/shard_map/ppermute | solution.py:234
